TPU v7x, 256 devices: a whole 4x4x8 slice. The times are simulated.
256 devices in a mesh: store: 16 (over z_lo, y), ctx: 16 (over x, z_hi, core).
Axes of the slice: x: 4, y: 4, z: 8 (z_hi: 2, z_lo: 4; z = z_hi * 4 + z_lo), core: 2. Of those that a mesh axis runs over, the one named last changes fastest.
Arguments:
- queries: bfloat16 [16384, 4096], P(('store', 'ctx')), may hold values from -24 to 24
- question_kv: bfloat16 [16384, 1024], P(('store', 'ctx')), may hold values from -6 to 6
- passage_kv: bfloat16 [2048, 64, 1024], P(('store', 'ctx')), may hold values from -6 to 6
- wanted: int32 [16, 16, 8], P(None, 'ctx'), may hold values from 0 to 2047, as said below
- live: int32 [16, 16], P(None, 'ctx'), may hold values from 6 to 8, as said below
Outputs:
- attended: bfloat16 [16384, 4096], P(('store', 'ctx'))
Inputs may be any that keep to these rules, and one draw needn't show every extreme that they name: Entry wanted[s, c, j] is stored on the device with store index wanted[s, c, j] // 128 and ctx index c; the 8 entries of one (s, c) lie on different store shards. Entries j < live[s, c] of wanted[s, c] are read, the others are not. In every request group some device reads all 8.
All inputs are finite; a program needn't handle non-finite values.
Results may differ from a plain program's by a relative error of at most 0.0038.
Values may be sent and summed in bfloat16 or wider, within the bound.
No kernel may reach another device: no remote copies, remote signals or barrier semaphores. Data moves between devices by JAX's collectives and lax.ppermute only.
A program may use at most 192 MiB of HBM per device.

v0:
```python
import math

import jax
import jax.numpy as jnp
from jax import lax
from jax.sharding import PartitionSpec as P

HQ = 32
KVH = 4
HD = 128


def attend_rows(
    query_block, row_pos, passage_keys, passage_vals, passage_flags, question_keys, question_vals
):
    score_scale = 1.0 / math.sqrt(query_block.shape[-1])
    passage_scores = (
        jnp.einsum("rpd,kd->rpk", query_block, passage_keys, preferred_element_type=jnp.float32)
        * score_scale
    )
    passage_scores = jnp.where(passage_flags[None, None, :], passage_scores, -1e30)
    question_scores = (
        jnp.einsum("rpd,kd->rpk", query_block, question_keys, preferred_element_type=jnp.float32)
        * score_scale
    )
    key_pos = lax.broadcasted_iota(jnp.int32, (1, question_keys.shape[0]), 1)
    causal = key_pos <= row_pos[:, None]
    question_scores = jnp.where(causal[:, None, :], question_scores, -1e30)
    row_max = jnp.maximum(jnp.max(passage_scores, axis=2), jnp.max(question_scores, axis=2))[
        :, :, None
    ]
    passage_weights = jnp.exp(passage_scores - row_max)
    question_weights = jnp.exp(question_scores - row_max)
    row_total = jnp.sum(passage_weights, axis=2) + jnp.sum(question_weights, axis=2)
    summed = jnp.einsum(
        "rpk,kd->rpd",
        passage_weights.astype(jnp.bfloat16),
        passage_vals,
        preferred_element_type=jnp.float32,
    )
    summed = summed + jnp.einsum(
        "rpk,kd->rpd",
        question_weights.astype(jnp.bfloat16),
        question_vals,
        preferred_element_type=jnp.float32,
    )
    return (summed / row_total[:, :, None]).astype(jnp.bfloat16)


def body(queries, question_kv, passage_kv, wanted, live):
    ctx_count = lax.axis_size("ctx")
    me_store = lax.axis_index("store")
    me_ctx = lax.axis_index("ctx")
    stored = passage_kv.shape[0]
    block_len = passage_kv.shape[1]
    kv_width = passage_kv.shape[2] // 2
    head_dim = HD
    per_group = HQ // KVH
    wanted_ids = wanted[:, 0, :]
    counts = live[:, 0]
    group_count = wanted_ids.shape[0]
    local_count = wanted_ids.shape[1]
    owner_ids = wanted_ids // (ctx_count * stored)
    place_ids = wanted_ids % stored
    live_mask = lax.broadcasted_iota(jnp.int32, wanted_ids.shape, 1) < counts[:, None]
    slot_range = lax.broadcasted_iota(jnp.int32, (group_count, local_count, stored), 2)
    chosen = (
        (owner_ids == me_store)[:, :, None]
        & live_mask[:, :, None]
        & (place_ids[:, :, None] == slot_range)
    )
    sender_pick = jnp.any(chosen, axis=1).astype(jnp.bfloat16)
    outgoing = jnp.einsum(
        "gb,btf->gtf", sender_pick, passage_kv, preferred_element_type=jnp.float32
    ).astype(jnp.bfloat16)
    my_owner = lax.dynamic_index_in_dim(owner_ids, me_store, 0, keepdims=False)
    my_used = lax.dynamic_index_in_dim(live_mask, me_store, 0, keepdims=False)
    sources = lax.broadcasted_iota(jnp.int32, (local_count, group_count), 1)
    choose = ((my_owner[:, None] == sources) & my_used[:, None]).astype(jnp.bfloat16)
    landed = jnp.einsum(
        "lg,gtf->ltf",
        choose,
        lax.all_to_all(outgoing, "store", split_axis=0, concat_axis=0, tiled=True),
        preferred_element_type=jnp.float32,
    ).astype(jnp.bfloat16)
    passage_rows = landed.reshape(local_count * block_len, 2 * kv_width)
    row_flags = jnp.repeat(my_used, block_len)
    query_count = queries.shape[0]
    every_rows, every_question, every_flags = (
        lax.all_gather(passage_rows, "ctx", axis=0, tiled=True),
        lax.all_gather(question_kv, "ctx", axis=0, tiled=True),
        lax.all_gather(row_flags.astype(jnp.bfloat16), "ctx", axis=0, tiled=True),
    )
    visible_rows = every_flags > 0
    row_pos = me_ctx * query_count + lax.broadcasted_iota(jnp.int32, (query_count,), 0)
    grouped = queries.reshape(query_count, KVH, per_group, head_dim)
    pieces = []
    for kv_head in range(KVH):
        key_start = kv_head * head_dim
        value_start = kv_width + kv_head * head_dim
        pieces.append(
            attend_rows(
                grouped[:, kv_head],
                row_pos,
                every_rows[:, key_start : key_start + head_dim],
                every_rows[:, value_start : value_start + head_dim],
                visible_rows,
                every_question[:, key_start : key_start + head_dim],
                every_question[:, value_start : value_start + head_dim],
            )
        )
    return jnp.concatenate(pieces, axis=1).reshape(query_count, HQ * head_dim)


def solution(mesh):
    return jax.shard_map(
        body,
        mesh=mesh,
        in_specs=(
            P(("store", "ctx"), None),
            P(("store", "ctx"), None),
            P(("store", "ctx"), None, None),
            P(None, "ctx", None),
            P(None, "ctx"),
        ),
        out_specs=P(("store", "ctx"), None),
        check_vma=False,
    )
```

profile of v0, /device:TPU:1, one launch (start us, length us, event | category | flops | bytes accessed | tf_op | source)
XLA Modules:
  0.0 401.6 jit_solution(1918799987297294380)
XLA Ops:
  6.5 0.8 add_select_fusion
  7.3 0.7 compare_and_fusion
  8.1 0.8 convolution_convert_fusion
  8.9 2.5 copy.116
  11.4 9.2 %all-to-all-start = ((bf16[16,64,1024]{2,1,0:T(8,128)(2,1)}), bf16[16,64,1024]{2,1,0:T(8,128)(2,1)S(1)}, u32[]{:S(2)}, u32[]{:S(2)}) async-start(bf16[16,64,1024]{2,1,0:T(8,128)(2,1)} %copy.116), calls=%async_computation | async-start | bytes 4194304 | tf_op jit(solution)/shard_map/all_to_all | solution.py:83
  20.7 0.7 all-gather.6.cloned.1.call-update
  21.4 0.2 dynamic-slice_reduce_fusion.1
  21.6 0.2 dynamic-slice_reduce_fusion
  21.8 43.1 %all-to-all-done = bf16[16,64,1024]{2,1,0:T(8,128)(2,1)S(1)} async-done(((bf16[16,64,1024]{2,1,0:T(8,128)(2,1)}), bf16[16,64,1024]{2,1,0:T(8,128)(2,1)S(1)}, u32[]{:S(2)}, u32[]{:S(2)}) %all-to-all-start) | async-done | bytes 2097184 | tf_op jit(solution)/shard_map/all_to_all | solution.py:83
  64.9 1.3 fusion.42
  66.2 1.6 copy.118
  67.9 33.0 %all-gather = bf16[16,1,512]{2,1,0:T(2,128)(2,1)S(1)} all-gather(bf16[1,1,512]{2,1,0:T(2,128)(2,1)S(1)} %reshape.152), channel_id=1, replica_groups=mesh['store'=16,'ctx'=16] {'ctx'}, dimensions={0}, use_global_device_ids=true | all-gather | bytes 17408 | tf_op jit(solution)/shard_map/all_gather | solution.py:92
  101.5 2.9 fusion.30
  104.4 1.4 fusion.94
  105.9 2.8 fusion.95
  108.7 159.6 %all-gather.4.cloned.1.call-done = bf16[8192,1024]{1,0:T(8,128)(2,1)} async-done(((bf16[512,1024]{1,0:T(8,128)(2,1)}), bf16[8192,1024]{1,0:T(8,128)(2,1)}) %all-gather.4.cloned.1.call-update) | async-done | bytes 16777232 | tf_op jit(solution)/shard_map/all_gather | solution.py:90
  268.3 8.9 %bitcast_reduce_fusion.3 = (f32[64,8]{0,1:T(8,128)S(1)}, f32[8192,64,8]{0,1,2:T(8,128)}) fusion(pred[8192]{0:T(1024)(128)(4,1)S(1)} %bitcast.227, bf16[64,1,8,128]{3,2,1,0:T(8,128)(2,1)S(1)} %get-tuple-element.23, bf16[8192,1024]{1,0:T(8,128)(2,1)} %all-gather.4.cloned.1.call-done), kind=kOutput, calls=%fused_computation.10 | convolution fusion | flops 1086324224 | bytes 19015680 | tf_op jit(solution)/shard_map/rpd,kd->rpk/dot_general | solution.py:18
  277.2 5.3 %fusion.34 = (f32[64,8]{1,0:T(8,128)S(1)}, f32[64,8]{1,0:T(8,128)S(1)}, f32[64,8]{1,0:T(8,128)S(1)}, f32[64,8]{1,0:T(8,128)S(1)}, f32[64,8,1024]{2,1,0:T(8,128)}) fusion(f32[64,8,1024]{2,1,0:T(8,128)} %get-tuple-element.29, f32[64,8]{1,0:T(8,128)S(1)} %copy.122, pred[64,1024]{1,0:T(8,128)(4,1)S(1)} %iota_compare_fusion, f32[64,8,1024]{2,1,0:T(8,128)} %fusion.95, ...), kind=kOutput, calls=%fused_computation.59 | convolution fusion | flops 141031424 | bytes 8888320 | tf_op jit(solution)/shard_map/rpd,kd->rpk/dot_general | solution.py:23
  282.7 9.7 %fusion.24 = f32[8192,64,8]{0,1,2:T(8,128)} fusion(bf16[8192,1024]{1,0:T(8,128)(2,1)} %all-gather.4.cloned.1.call-done, bf16[64,1,8,128]{3,2,1,0:T(8,128)(2,1)S(1)} %get-tuple-element.24), kind=kOutput, calls=%fused_computation.34 | convolution fusion | flops 1073741824 | bytes 19005440 | tf_op jit(solution)/shard_map/rpd,kd->rpk/dot_general | solution.py:18
  292.4 9.6 %fusion.25 = f32[8192,64,8]{0,1,2:T(8,128)} fusion(bf16[8192,1024]{1,0:T(8,128)(2,1)} %all-gather.4.cloned.1.call-done, bf16[64,1,8,128]{3,2,1,0:T(8,128)(2,1)S(1)} %get-tuple-element.21), kind=kOutput, calls=%fused_computation.37 | convolution fusion | flops 1073741824 | bytes 19005440 | tf_op jit(solution)/shard_map/rpd,kd->rpk/dot_general | solution.py:18
  302.1 25.6 %fusion.4 = (f32[64,8]{0,1:T(8,128)S(1)}, f32[64,8]{0,1:T(8,128)S(1)}, f32[64,8]{0,1:T(8,128)S(1)}, f32[64,8]{0,1:T(8,128)S(1)}, f32[8192,64,8]{0,1,2:T(8,128)}) fusion(f32[8192,64,8]{0,1,2:T(8,128)} %get-tuple-element.27, f32[64,8]{0,1:T(8,128)S(1)} %max.28, pred[8192]{0:T(1024)(128)(4,1)S(1)} %bitcast.228, f32[8192,64,8]{0,1,2:T(8,128)} %fusion.25, ...), kind=kOutput, calls=%fused_computation.16 | convolution fusion | flops 1128265728 | bytes 69355520 | tf_op jit(solution)/shard_map/rpd,kd->rpk/dot_general | solution.py:18
  328.0 19.8 %fusion.6 = (f32[64,8]{0,1:T(8,128)S(1)}, f32[64,8]{0,1:T(8,128)S(1)}, f32[64,8]{0,1:T(8,128)S(1)}) fusion(f32[8192,64,8]{0,1,2:T(8,128)} %get-tuple-element.30, f32[64,8]{0,1:T(8,128)S(1)} %max.29, pred[8192]{0:T(1024)(128)(4,1)S(1)} %bitcast.229, f32[64,8]{0,1:T(8,128)S(1)} %max.30, f32[8192,64,8]{0,1,2:T(8,128)} %fusion.25, f32[64,8]{0,1:T(8,128)S(1)} %max.31, ...), kind=kLoop, calls=%fused_computation.18 | loop fusion | flops 50330112 | bytes 50352128 | tf_op jit(solution)/shard_map/reduce_sum | solution.py:34
  347.8 2.0 fusion.36
  350.0 2.5 fusion.88
  352.5 1.7 fusion.84
  354.2 1.8 fusion.82
  356.0 1.7 fusion.86
  357.7 9.9 %fusion.78 = bf16[64,8,128]{2,0,1:T(8,128)(2,1)S(1)} fusion(bf16[8192,1024]{1,0:T(8,128)(2,1)} %all-gather.4.cloned.1.call-done, f32[8192,64,8]{0,1,2:T(8,128)} %get-tuple-element.27, f32[64,8]{0,1:T(8,128)S(1)} %max.28, pred[8192]{0:T(1024)(128)(4,1)S(1)} %bitcast.230, f32[64,8,128]{2,1,0:T(8,128)S(1)} %fusion.88, f32[64,8]{0,1:T(8,128)S(1)} %add.76), kind=kOutput, calls=%fused_computation.79 | convolution fusion | flops 1090715648 | bytes 19279872 | tf_op jit(solution)/shard_map/rpk,kd->rpd/dot_general | solution.py:35
  367.7 10.1 %fusion.72 = bf16[64,8,128]{2,0,1:T(8,128)(2,1)S(1)} fusion(bf16[8192,1024]{1,0:T(8,128)(2,1)} %all-gather.4.cloned.1.call-done, f32[8192,64,8]{0,1,2:T(8,128)} %get-tuple-element.30, f32[64,8]{0,1:T(8,128)S(1)} %max.29, pred[8192]{0:T(1024)(128)(4,1)S(1)} %bitcast.231, f32[64,8,128]{2,1,0:T(8,128)S(1)} %fusion.86, f32[64,8]{0,1:T(8,128)S(1)} %add.78), kind=kOutput, calls=%fused_computation.77 | convolution fusion | flops 1090715648 | bytes 19279872 | tf_op jit(solution)/shard_map/rpk,kd->rpd/dot_general | solution.py:35
  377.8 10.3 %fusion.66 = bf16[64,8,128]{2,0,1:T(8,128)(2,1)S(1)} fusion(bf16[8192,1024]{1,0:T(8,128)(2,1)} %all-gather.4.cloned.1.call-done, f32[8192,64,8]{0,1,2:T(8,128)} %fusion.25, f32[64,8]{0,1:T(8,128)S(1)} %max.30, pred[8192]{0:T(1024)(128)(4,1)S(1)} %bitcast.232, f32[64,8,128]{2,1,0:T(8,128)S(1)} %fusion.84, f32[64,8]{0,1:T(8,128)S(1)} %add.80), kind=kOutput, calls=%fused_computation.75 | convolution fusion | flops 1090715648 | bytes 19279872 | tf_op jit(solution)/shard_map/rpk,kd->rpd/dot_general | solution.py:35
  388.2 5.3 %fusion.60 = bf16[64,8,128]{2,0,1:T(8,128)(2,1)S(1)} fusion(bf16[8192,1024]{1,0:T(8,128)(2,1)} %all-gather.4.cloned.1.call-done, f32[8192,64,8]{0,1,2:T(8,128)S(1)} %bitcast.218, f32[64,8]{0,1:T(8,128)S(1)} %max.31, pred[8192]{0:T(1024)(128)(4,1)S(1)} %bitcast.233, f32[64,8,128]{2,1,0:T(8,128)S(1)} %fusion.82, f32[64,8]{0,1:T(8,128)S(1)} %add.82), kind=kOutput, calls=%fused_computation.73 | convolution fusion | flops 1090715648 | bytes 19279872 | tf_op jit(solution)/shard_map/rpk,kd->rpd/dot_general | solution.py:35
  393.5 0.9 copy_bitcast_fusion
  (57 shorter events, 1.6 us)
Async XLA Ops:
  6.5 1.5 copy-start
  11.4 53.5 %all-to-all-start = ((bf16[16,64,1024]{2,1,0:T(8,128)(2,1)}), bf16[16,64,1024]{2,1,0:T(8,128)(2,1)S(1)}, u32[]{:S(2)}, u32[]{:S(2)}) async-start(bf16[16,64,1024]{2,1,0:T(8,128)(2,1)} %copy.116), calls=%async_computation | async-start | bytes 4194304 | tf_op jit(solution)/shard_map/all_to_all | solution.py:83
  20.6 80.9 %all-gather.6.cloned.1.call-start = ((), (), s32[]{:S(2)}) async-start(), calls=%async_computation.2 | async-start | bytes 2228224 | tf_op jit(solution)/shard_map/all_gather | solution.py:91
  21.4 246.9 %all-gather.4.cloned.1.call-start = ((), (), s32[]{:S(2)}) async-start(), calls=%async_computation.1 | async-start | bytes 17825792 | tf_op jit(solution)/shard_map/all_gather | solution.py:90
  66.2 35.0 %copy-start.6 = (bf16[64,4096]{1,0:T(8,128)(2,1)S(1)}, bf16[64,4096]{1,0:T(8,128)(2,1)}, u32[]{:S(2)}) copy-start(bf16[64,4096]{1,0:T(8,128)(2,1)} %param.5) | copy-start | bytes 1572868
  328.0 19.8 %copy-start.2 = (f32[64,8,1024]{2,1,0:T(8,128)S(1)}, f32[64,8,1024]{2,1,0:T(8,128)}, u32[]{:S(2)}) copy-start(f32[64,8,1024]{2,1,0:T(8,128)} %fusion.95) | copy-start | bytes 6291460
  328.0 19.8 %copy-start.4 = (f32[64,8,1024]{2,1,0:T(8,128)S(1)}, f32[64,8,1024]{2,1,0:T(8,128)}, u32[]{:S(2)}) copy-start(f32[64,8,1024]{2,1,0:T(8,128)} %get-tuple-element.31) | copy-start | bytes 6291460
  350.0 2.5 copy-start.3
  354.2 1.8 copy-start.5
  367.7 20.5 %slice-start = ((s8[16777216]{0:T(1024)(128)(4,1)}), s8[4194304]{0:T(1024)(128)(4,1)S(1)}, s32[]{:S(2)}) async-start(s8[16777216]{0:T(1024)(128)(4,1)} %bitcast.217), calls=%async_computation.3 | async-start | bytes 8388608
  367.7 20.5 %slice-start.1 = ((s8[16777216]{0:T(1024)(128)(4,1)}), s8[4194304]{0:T(1024)(128)(4,1)S(1)}, s32[]{:S(2)}) async-start(s8[16777216]{0:T(1024)(128)(4,1)} %bitcast.217), calls=%async_computation.4 | async-start | bytes 8388608
  377.8 10.4 %slice-start.2 = ((s8[16777216]{0:T(1024)(128)(4,1)}), s8[4194304]{0:T(1024)(128)(4,1)S(1)}, s32[]{:S(2)}) async-start(s8[16777216]{0:T(1024)(128)(4,1)} %bitcast.217), calls=%async_computation.5 | async-start | bytes 8388608
  377.8 10.4 %slice-start.3 = ((s8[16777216]{0:T(1024)(128)(4,1)}), s8[4194304]{0:T(1024)(128)(4,1)S(1)}, s32[]{:S(2)}) async-start(s8[16777216]{0:T(1024)(128)(4,1)} %bitcast.217), calls=%async_computation.6 | async-start | bytes 8388608
  388.2 6.1 %copy-start.1 = (bf16[8,64,1024]{2,1,0:T(8,128)(2,1)S(1)}, bf16[8,64,1024]{2,1,0:T(8,128)(2,1)}, u32[]{:S(2)}) copy-start(bf16[8,64,1024]{2,1,0:T(8,128)(2,1)} %param.7) | copy-start | bytes 3145732
Sparse Core Ops, SparseCore 0:
  24.1 63.9 all-gather.5
  90.8 177.4 all-gather.3
where the time goes:
time: 407 us; the launch traced here: 402 us
  waiting for transfers between devices  203 us (50%)
  matrix products  112 us (28%)
  blocking collectives  33 us (8%)
  other arithmetic  24.4 us (6%)
  between operations  14.2 us (3%)
  starting transfers between devices  9.27 us (2%)
  local copies, waits for them, and re-layouts  5.67 us (1%)
    all_gather x1, waiting for transfers between devices, body(): lax.all_gather(passage_rows, 'ctx', axis=0, tiled=True)  160 us
    dot_general x4, matrix products, attend_rows(): jnp.einsum('rpd,kd->rpk', query_block, passage_keys, preferred_element_ty...  53.8 us
    all_to_all x1, waiting for transfers between devices, body(): lax.all_to_all(outgoing, 'store', split_axis=0, concat_axis=0, tiled=True)  43.1 us
    dot_general x4, matrix products, attend_rows(): jnp.einsum('rpk,kd->rpd', passage_weights.astype(jnp.bfloat16), passage_v...  35.6 us
    all_gather x1, blocking collectives, body(): lax.all_gather(row_flags.astype(jnp.bfloat16), 'ctx', axis=0, tiled=True)  33 us
    reduce_sum x1, other arithmetic, attend_rows(): jnp.sum(passage_weights, axis=2) + jnp.sum(question_weights, axis=2)  19.8 us
    dot_general x4, matrix products, attend_rows(): jnp.einsum('rpd,kd->rpk', query_block, question_keys, preferred_element_t...  12.4 us
    all_to_all x1, starting transfers between devices, body(): lax.all_to_all(outgoing, 'store', split_axis=0, concat_axis=0, tiled=True)  9.19 us
  transfers between devices with their start and end apart: 3, of which 2 were waited for; matrix products, arithmetic and copies ran while one was open for 3% of the time, Pallas kernels for 0%

commit v1 on v0

v1 whole, which is shorter than its diff:
```python
import functools
import math

import jax
import jax.numpy as jnp
from jax import lax
from jax.experimental import pallas as pl
from jax.experimental.pallas import tpu as pltpu
from jax.sharding import Mesh, PartitionSpec as P

HQ = 32
KVH = 4
HD = 128
GROUP_HEADS = HQ // KVH
BLK = 64
GROUPS = 16
LOCAL = 8
STORED = 8
ROWS = 64
INFO_ROWS = 16
PIECE_ROWS = ROWS + INFO_ROWS
QCOLS = GROUP_HEADS * HD
PIECE = QCOLS + 2 * HD
HEAD_ROWS = 4 * ROWS
ALL_ROWS = GROUP_HEADS * HEAD_ROWS
STEP_HEADS = 2
STEP_ROWS = STEP_HEADS * HEAD_ROWS
EXP2_SCALE = math.log2(math.e) / math.sqrt(HD)
LOWEST = -1e30
CHUNKS = (48, 16)
KEY_TILE = 1024

AXES = ("zlo", "y", "x", "zhi", "core")
HEAD_AXES = ("zhi", "core")
SEND_AXES = ("zlo", "y", "zhi", "core")

VMEM = pl.BlockSpec(memory_space=pltpu.VMEM)
SMEM = pl.BlockSpec(memory_space=pltpu.SMEM)
BF16 = jnp.bfloat16


def params(mib=40):
    return pltpu.CompilerParams(vmem_limit_bytes=mib * 2**20)


def cost(flops, size):
    return pl.CostEstimate(flops=flops, bytes_accessed=size, transcendentals=0)


def bf16_shape(*dims):
    return jax.ShapeDtypeStruct(dims, BF16)


def columns(index, width):
    return pl.ds(pl.multiple_of(index * width, width), width)


def split_kernel(head_ref, q_ref, kv_ref, info_ref, *outs):
    for offset, out in enumerate(outs):
        head = head_ref[0] ^ offset
        out[:ROWS, :QCOLS] = q_ref[:, columns(head, QCOLS)]
        out[ROWS:, :QCOLS] = jnp.zeros((INFO_ROWS, QCOLS), BF16)
        out[:ROWS, QCOLS : QCOLS + HD] = kv_ref[:, columns(head, HD)]
        out[:ROWS, QCOLS + HD :] = kv_ref[:, columns(KVH + head, HD)]
        out[ROWS:, QCOLS:] = info_ref[...]


def split_queries(head, queries, question_kv, info):
    return pl.pallas_call(
        split_kernel,
        out_shape=[bf16_shape(PIECE_ROWS, PIECE)] * 4,
        in_specs=[SMEM, VMEM, VMEM, VMEM],
        out_specs=[VMEM] * 4,
        compiler_params=params(16),
        cost_estimate=cost(0, 1 << 20),
    )(head, queries, question_kv, info)


def select_kernel(slot_ref, stored_ref, *outs):
    def one(group, carry):
        slot = slot_ref[group]
        start = 0
        for size, out in zip(CHUNKS, outs):
            tokens = slice(start, start + size)
            for head in range(KVH):
                keys = slice(head * HD, (head + 1) * HD)
                values = slice((KVH + head) * HD, (KVH + head + 1) * HD)
                out[group * KVH + head, :, :HD] = stored_ref[slot, tokens, keys]
                out[group * KVH + head, :, HD:] = stored_ref[slot, tokens, values]
            start += size
        return carry

    lax.fori_loop(0, GROUPS, one, 0)


def select_blocks(slots, stored):
    return pl.pallas_call(
        select_kernel,
        out_shape=[bf16_shape(GROUPS * KVH, size, 2 * HD) for size in CHUNKS],
        in_specs=[SMEM, VMEM],
        out_specs=[VMEM] * len(CHUNKS),
        compiler_params=params(16),
        cost_estimate=cost(0, 3 << 20),
    )(slots, stored)


def collect_kernel(p0, p1, p2, p3, question, info):
    for offset, piece in enumerate((p0, p1, p2, p3)):
        rows = slice(offset * PIECE_ROWS, (offset + 1) * PIECE_ROWS)
        question[rows, :] = piece[:, QCOLS:]
        told = piece[ROWS:, QCOLS:].astype(jnp.float32)
        info[offset : offset + 1, :] = told[:1, :].astype(jnp.int32)


def collect(pieces):
    return pl.pallas_call(
        collect_kernel,
        out_shape=[
            bf16_shape(4 * PIECE_ROWS, 2 * HD),
            jax.ShapeDtypeStruct((4, 2 * HD), jnp.int32),
        ],
        in_specs=[VMEM] * 4,
        out_specs=[VMEM] * 2,
        compiler_params=params(16),
        cost_estimate=cost(0, 1 << 20),
    )(*pieces)


def pack_kernel(slot_ref, flag_ref, landed_ref, out_ref):
    tokens = landed_ref.shape[1]

    def one(entry, carry):
        rows = columns(entry, tokens)
        out_ref[rows, :] = landed_ref[slot_ref[entry]]

        @pl.when(flag_ref[entry] == 0)
        def _():
            out_ref[rows, HD:] = jnp.zeros((tokens, HD), BF16)

        return carry

    lax.fori_loop(0, 4 * LOCAL, one, 0)


def pack_blocks(slots, flags, landed):
    tokens = landed.shape[1]
    return pl.pallas_call(
        pack_kernel,
        out_shape=bf16_shape(4 * LOCAL * tokens, 2 * HD),
        in_specs=[SMEM, SMEM, VMEM],
        out_specs=VMEM,
        compiler_params=params(16),
        cost_estimate=cost(0, 3 << 20),
    )(slots, flags, landed)


def step(query, keys, values, state_max, state_sum, mask=None):
    scores = lax.dot_general(
        query, keys, (((1,), (1,)), ((), ())), preferred_element_type=jnp.float32
    )
    if mask is not None:
        scores = jnp.where(mask, scores, LOWEST)
    new_max = jnp.maximum(state_max, jnp.max(scores, axis=1, keepdims=True))
    scale = jnp.exp2((state_max - new_max) * EXP2_SCALE)
    weights = jnp.exp2((scores - new_max[:, :1]) * EXP2_SCALE).astype(jnp.bfloat16)
    summed = jnp.dot(weights, values, preferred_element_type=jnp.float32)
    return new_max, state_sum * jnp.concatenate([scale, scale], axis=1) + summed


def question_kernel(
    place_ref, p0, p1, p2, p3, left, right, far, q_out, max_out, sum_out, flag_out, held
):
    head, column = place_ref[0], place_ref[1]
    ones = jnp.ones((HEAD_ROWS, HD), BF16)
    entry = lax.broadcasted_iota(jnp.int32, (LOCAL, HD), 0).astype(jnp.float32)

    def hold(slot, offset, piece, row, start):
        held[slot, offset * ROWS : (offset + 1) * ROWS, :] = piece[row : row + ROWS, start:]
        info = piece[row + ROWS : row + PIECE_ROWS, start + HD :].astype(jnp.float32)
        first = (slot * 4 + offset) * LOCAL
        flag_out[first : first + LOCAL, :] = (entry < info[:1, :]).astype(jnp.float32)

    for offset, piece in enumerate((p0, p1, p2, p3)):
        hold(0, offset, piece, 0, QCOLS)
        for h in range(GROUP_HEADS):
            start = h * HEAD_ROWS + offset * ROWS
            q_out[start : start + ROWS, :] = piece[:ROWS, h * HD : (h + 1) * HD]
        for slot, other in enumerate((left, right, far)):
            hold(slot + 1, offset, other, offset * PIECE_ROWS, 0)

    def positions(axis, shape):
        index = lax.broadcasted_iota(jnp.int32, shape, axis)
        return ((index // ROWS) ^ head) * ROWS + index % ROWS

    shape = (HEAD_ROWS, HEAD_ROWS)
    mask = positions(1, shape) <= positions(0, shape)
    low = jnp.full((HEAD_ROWS, HD), LOWEST, jnp.float32)
    zero = jnp.zeros((HEAD_ROWS, 2 * HD), jnp.float32)

    def first(h, carry):
        rows = columns(h, HEAD_ROWS)
        values = jnp.concatenate([held[0, :, HD:], ones], axis=1)
        max_out[rows, :], sum_out[rows, :] = step(
            q_out[rows, :], held[0, :, :HD], values, low, zero, mask
        )
        return carry

    lax.fori_loop(0, GROUP_HEADS, first, 0)
    for least, slot in ((1, 1), (2, 3), (3, 2)):

        @pl.when(column >= least)
        def _(slot=slot):
            def more(h, carry):
                rows = columns(h, HEAD_ROWS)
                values = jnp.concatenate([held[slot, :, HD:], ones], axis=1)
                max_out[rows, :], sum_out[rows, :] = step(
                    q_out[rows, :], held[slot, :, :HD], values, max_out[rows, :], sum_out[rows, :]
                )
                return carry

            lax.fori_loop(0, GROUP_HEADS, more, 0)


STATE = (
    jax.ShapeDtypeStruct((ALL_ROWS, HD), jnp.float32),
    jax.ShapeDtypeStruct((ALL_ROWS, 2 * HD), jnp.float32),
)


def question_part(place, pieces, left, right, far):
    flags = jax.ShapeDtypeStruct((16 * LOCAL, HD), jnp.float32)
    return pl.pallas_call(
        question_kernel,
        out_shape=[bf16_shape(ALL_ROWS, HD), *STATE, flags],
        in_specs=[SMEM] + [VMEM] * 7,
        out_specs=[VMEM] * 4,
        scratch_shapes=[pltpu.VMEM((4, HEAD_ROWS, 2 * HD), BF16)],
        compiler_params=params(),
        cost_estimate=cost(4 * ALL_ROWS * 1024 * HD, 4 << 20),
    )(place, *pieces, left, right, far)


def passage_kernel(layout, last, flag_ref, q_ref, max_ref, sum_ref, *refs):
    tiles, refs = refs[: len(layout)], refs[len(layout) :]
    outs, value_refs = refs[: -len(layout)], refs[-len(layout) :]
    for (first, count), tile, value_ref in zip(layout, tiles, value_refs):
        tokens = tile.shape[0] // count
        value_ref[:, :HD] = tile[:, HD:]
        for block in range(count):
            flag = jnp.broadcast_to(flag_ref[first + block : first + block + 1, :], (tokens, HD))
            value_ref[block * tokens : (block + 1) * tokens, HD:] = flag.astype(BF16)

    def one(t, carry):
        rows = columns(t, STEP_ROWS)
        query, state_max, state_sum = q_ref[rows, :], max_ref[rows, :], sum_ref[rows, :]
        for tile, value_ref in zip(tiles, value_refs):
            size = tile.shape[0]
            for start in range(0, size, KEY_TILE):
                stop = min(start + KEY_TILE, size)
                state_max, state_sum = step(
                    query, tile[start:stop, :HD], value_ref[start:stop, :], state_max, state_sum
                )
        if last:
            result = (state_sum[:, :HD] / state_sum[:, HD:]).astype(BF16)
            for u in range(STEP_HEADS):
                for offset, out in enumerate(outs):
                    start = u * HEAD_ROWS + offset * ROWS
                    out[:, columns(t * STEP_HEADS + u, HD)] = result[start : start + ROWS, :]
        else:
            outs[0][rows, :] = state_max
            outs[1][rows, :] = state_sum
        return carry

    lax.fori_loop(0, GROUP_HEADS // STEP_HEADS, one, 0)


def passage_part(flags, query, state, tiles, layout, last):
    shapes = [bf16_shape(ROWS, QCOLS)] * 4 if last else list(STATE)
    keys = sum(tile.shape[0] for tile in tiles)
    return pl.pallas_call(
        functools.partial(passage_kernel, layout, last),
        out_shape=shapes,
        in_specs=[VMEM] * (4 + len(tiles)),
        out_specs=[VMEM] * len(shapes),
        scratch_shapes=[pltpu.VMEM((tile.shape[0], 2 * HD), BF16) for tile in tiles],
        compiler_params=params(),
        cost_estimate=cost(4 * ALL_ROWS * keys * HD * 2, 8 << 20),
    )(flags, query, *state, *tiles)


def join_kernel(head_ref, *refs):
    out = refs[-1]
    for offset, piece in enumerate(refs[:-1]):
        out[:, columns(head_ref[0] ^ offset, QCOLS)] = piece[...]


def join_outputs(head, pieces):
    return pl.pallas_call(
        join_kernel,
        out_shape=bf16_shape(ROWS, HQ * HD),
        in_specs=[SMEM] + [VMEM] * 4,
        out_specs=VMEM,
        compiler_params=params(16),
        cost_estimate=cost(0, 1 << 20),
    )(head, *pieces)


def swap_heads(pieces):
    moved = [pieces[0]]
    for offset in range(1, 4):
        pairs = [(i, i ^ offset) for i in range(4)]
        moved.append(lax.ppermute(pieces[offset], HEAD_AXES, pairs))
    return moved


def along(axis, value, hops):
    return lax.ppermute(value, axis, [(i, (i + hops) % 4) for i in range(4)])


def ints(*values):
    return jnp.stack([jnp.asarray(value, jnp.int32) for value in values])


def body(queries, question_kv, passage_kv, wanted, live):
    x = lax.axis_index("x")
    store = lax.axis_index("zlo") * 4 + lax.axis_index("y")
    head = lax.axis_index("zhi") * 2 + lax.axis_index("core")

    wanted_ids = wanted[:, 0, :]
    owner_ids = wanted_ids // (GROUPS * STORED)
    slots = jnp.sum(jnp.where(owner_ids == store, wanted_ids % STORED, 0), axis=1)
    slots = slots.astype(jnp.int32)

    owners = lax.dynamic_index_in_dim(owner_ids, store, 0, keepdims=True)
    count = lax.dynamic_index_in_dim(live, store, 0, keepdims=True)
    info = jnp.concatenate(
        [jnp.pad(owners, ((0, 0), (0, HD - LOCAL))), jnp.broadcast_to(count, (1, HD))], axis=1
    )
    info = jnp.broadcast_to(info.astype(BF16), (INFO_ROWS, 2 * HD))
    outgoing = select_blocks(slots, passage_kv)
    pieces = swap_heads(split_queries(ints(head), queries, question_kv, info))
    *outgoing, p1, p2, p3 = lax.optimization_barrier((*outgoing, *pieces[1:]))
    pieces = [pieces[0], p1, p2, p3]

    question, near = collect(pieces)
    owners, counts = near[:, :LOCAL], near[:, HD : HD + 1]
    offset = lax.broadcasted_iota(jnp.int32, (4, LOCAL), 0)
    slot = owners * KVH + (head ^ offset)
    read = lax.broadcasted_iota(jnp.int32, (4, LOCAL), 1) < counts
    landed_slots = jnp.where(read, slot, slot[:, :1]).reshape(-1)
    landed_flags = read.astype(jnp.int32).reshape(-1)

    query, *state, flags = question_part(
        ints(head, x),
        pieces,
        along("x", question, 1),
        along("x", question, 3),
        along("x", question, 2),
    )

    quarter, half = 4 * LOCAL, 2 * LOCAL
    for chunk, tokens in enumerate(CHUNKS):
        last = chunk == len(CHUNKS) - 1
        landed = lax.all_to_all(outgoing[chunk], SEND_AXES, 0, 0, tiled=True)
        landed, *state = lax.optimization_barrier((landed, *state))
        own = pack_blocks(landed_slots, landed_flags, landed)
        left, right = along("x", own, 1), along("x", own, 3)
        far = (along("x", left[: half * tokens], 1), along("x", right[half * tokens :], 3))
        near_layout = ((quarter, quarter), (2 * quarter, quarter))
        far_layout = ((3 * quarter, half), (3 * quarter + half, half))
        state = passage_part(flags, query, state, (own,), ((0, quarter),), False)
        if last:
            layout = near_layout + far_layout
            state = passage_part(flags, query, state, (left, right, *far), layout, True)
        else:
            state = passage_part(flags, query, state, (left, right), near_layout, False)
            state = passage_part(flags, query, state, far, far_layout, False)

    return join_outputs(ints(head), swap_heads(state))


def solution(mesh):
    fine = Mesh(mesh.devices.reshape(4, 4, 4, 2, 2), AXES)
    store, ctx = ("zlo", "y"), ("x", "zhi", "core")
    every = store + ctx
    return jax.shard_map(
        body,
        mesh=fine,
        in_specs=(
            P(every, None),
            P(every, None),
            P(every, None, None),
            P(None, ctx, None),
            P(None, ctx),
        ),
        out_specs=P(every, None),
        check_vma=False,
    )
```

time: 407 us -> 177 us (0.43); the launches traced: 402 us -> 176 us
  waiting for transfers between devices: 203 us -> 56.4 us
  matrix products: 112 us -> 0 us
  Pallas kernels: 0 us -> 48.5 us
  starting transfers between devices: 9.27 us -> 53.7 us
  blocking collectives: 33 us -> 0 us
  other arithmetic: 24.4 us -> 3.08 us
  between operations: 14.2 us -> 0.24 us
  local copies, waits for them, and re-layouts: 5.67 us -> 14 us
    all_gather x2 -> x0, waiting for transfers between devices: 160 us -> none  [the longest x1 160 us: body(): lax.all_gather(passage_rows, 'ctx', axis=0, tiled=True)]
    dot_general x18 -> x0, matrix products: 112 us -> none  [the longest x4 53.8 us: attend_rows(): jnp.einsum('rpd,kd->rpk', query_block, passage_keys, preferred_element_ty...]
    pallas_call x0 -> x12, Pallas kernels: none -> 48.5 us  [the longest x5 39.2 us: passage_part(): pl.pallas_call(functools.partial(passage_kernel, layout, last), out_shape...]
    ppermute x0 -> x17, waiting for transfers between devices: none -> 33.3 us  [the longest x6 18.4 us: swap_heads(): moved.append(lax.ppermute(pieces[offset], HEAD_AXES, pairs))]
    all_gather x1 -> x0, blocking collectives: 33 us -> none  [body(): lax.all_gather(row_flags.astype(jnp.bfloat16), 'ctx', axis=0, tiled=True)]
    ppermute x0 -> x17, starting transfers between devices: none -> 32 us  [the longest x6 16.4 us: swap_heads(): moved.append(lax.ppermute(pieces[offset], HEAD_AXES, pairs))]
    reduce_sum x2 -> x1, other arithmetic: 21.8 us -> 0.71 us  [body(): jnp.sum(jnp.where(owner_ids == store, wanted_ids % STORED, 0), axis=1)]
    all_to_all x1 -> x2, waiting for transfers between devices: 43.1 us -> 23.1 us  [body(): landed = lax.all_to_all(outgoing[chunk], SEND_AXES, 0, 0, tiled=True)]
  transfers between devices with their start and end apart: 3 -> 19, of which waited for: 2 -> 9; matrix products, arithmetic and copies ran while one was open for 3% -> 2% of each run, Pallas kernels for 0% -> 22%
where the time goes in v1:
time: 177 us; the launch traced here: 176 us
  waiting for transfers between devices  56.4 us (32%)
  starting transfers between devices  53.7 us (30%)
  Pallas kernels  48.5 us (27%)
  local copies, waits for them, and re-layouts  14 us (8%)
  other arithmetic  3.08 us (2%)
    pallas_call x5, Pallas kernels, passage_part(): pl.pallas_call(functools.partial(passage_kernel, layout, last), out_shape...  39.2 us
    all_to_all x2, waiting for transfers between devices, body(): landed = lax.all_to_all(outgoing[chunk], SEND_AXES, 0, 0, tiled=True)  23.1 us
    all_to_all x2, starting transfers between devices, body(): landed = lax.all_to_all(outgoing[chunk], SEND_AXES, 0, 0, tiled=True)  21.7 us
    ppermute x6, waiting for transfers between devices, swap_heads(): moved.append(lax.ppermute(pieces[offset], HEAD_AXES, pairs))  18.4 us
    ppermute x6, starting transfers between devices, swap_heads(): moved.append(lax.ppermute(pieces[offset], HEAD_AXES, pairs))  16.4 us
    ppermute x11, starting transfers between devices, along(): return lax.ppermute(value, axis, [(i, (i + hops) % 4) for i in range(4)])  15.6 us
    ppermute x11, waiting for transfers between devices, along(): return lax.ppermute(value, axis, [(i, (i + hops) % 4) for i in range(4)])  14.9 us
    unnamed x24, local copies, waits for them, and re-layouts  11.5 us
  transfers between devices with their start and end apart: 19, of which 9 were waited for; matrix products, arithmetic and copies ran while one was open for 2% of the time, Pallas kernels for 22%

profile of v1, /device:TPU:1, one launch (start us, length us, event | category | flops | bytes accessed | tf_op | source)
XLA Modules:
  0.0 175.9 jit_solution(5553935851525977120)
XLA Ops:
  4.8 3.3 %collective-permute-start = (bf16[80,1280]{1,0:T(8,128)(2,1)S(1)}, bf16[80,1280]{1,0:T(8,128)(2,1)S(1)}, u32[]{:S(2)}, u32[]{:S(2)}) collective-permute-start(bf16[80,1280]{1,0:T(8,128)(2,1)S(1)} %get-tuple-element.43), channel_id=1, source_target_pairs={{0,1},{1,0},{2,3},{3,2},{4,5},{5,4},{6,7},{7,6},{8,9},{9,8},{10,11... | collective-permute-start | bytes 614408 | tf_op jit(solution)/shard_map/ppermute | solution.py:312
  8.1 5.2 %collective-permute-start.1 = (bf16[80,1280]{1,0:T(8,128)(2,1)S(1)}, bf16[80,1280]{1,0:T(8,128)(2,1)S(1)}, u32[]{:S(2)}, u32[]{:S(2)}) collective-permute-start(bf16[80,1280]{1,0:T(8,128)(2,1)S(1)} %get-tuple-element.44), channel_id=1, source_target_pairs={{0,2},{1,3},{2,0},{3,1},{4,6},{5,7},{6,4},{7,5},{8,10},{9,11},{10,... | collective-permute-start | bytes 614408 | tf_op jit(solution)/shard_map/ppermute | solution.py:312
  15.0 2.3 %shard_map.56 = (bf16[64,48,256]{2,1,0:T(8,128)(2,1)}, bf16[64,16,256]{2,1,0:T(8,128)(2,1)}) custom-call(s32[16]{0:T(128)S(1)} %get-tuple-element.75.slot_ref, bf16[8,64,1024]{2,1,0:T(8,128)(2,1)S(1)} %copy-done), custom_call_target="tpu_custom_call" | custom-call | bytes 3145728 | tf_op jit(solution)/shard_map/pallas_call | solution.py:97
  17.4 1.3 collective-permute-done.1.p2
  18.7 6.9 %collective-permute-done.2.p3 = bf16[80,1280]{1,0:T(8,128)(2,1)S(1)} collective-permute-done((bf16[80,1280]{1,0:T(8,128)(2,1)S(1)}, bf16[80,1280]{1,0:T(8,128)(2,1)S(1)}, u32[]{:S(2)}, u32[]{:S(2)}) %collective-permute-start.2) | collective-permute-done | bytes 204832 | tf_op jit(solution)/shard_map/ppermute | solution.py:312
  25.6 16.2 %all-to-all-start.1 = ((bf16[64,48,256]{2,1,0:T(8,128)(2,1)}), bf16[64,48,256]{2,1,0:T(8,128)(2,1)S(1)}, u32[]{:S(2)}, u32[]{:S(2)}) async-start(bf16[64,48,256]{2,1,0:T(8,128)(2,1)} %get-tuple-element.53), calls=%async_computation.1 | async-start | bytes 3145728 | tf_op jit(solution)/shard_map/all_to_all | solution.py:364
  41.8 1.3 collective-permute-start.3
  43.1 1.5 collective-permute-start.4
  44.6 1.5 collective-permute-start.5
  46.8 1.7 collective-permute-done.3.left
  48.5 4.5 %collective-permute-done.5.far = bf16[320,256]{1,0:T(8,128)(2,1)S(1)} collective-permute-done((bf16[320,256]{1,0:T(8,128)(2,1)S(1)}, bf16[320,256]{1,0:T(8,128)(2,1)S(1)}, u32[]{:S(2)}, u32[]{:S(2)}) %collective-permute-start.5) | collective-permute-done | bytes 163872 | tf_op jit(solution)/shard_map/ppermute | solution.py:317
  53.0 4.1 %shard_map.58 = (bf16[2048,128]{1,0:T(8,128)(2,1)S(1)}, f32[2048,128]{1,0:T(8,128)S(1)}, f32[2048,256]{1,0:T(8,128)S(1)}, f32[128,128]{1,0:T(8,128)S(1)}) custom-call(s32[2]{0:T(128)S(1)} %pad_add_fusion.place_ref, bf16[80,1280]{1,0:T(8,128)(2,1)S(1)} %get-tuple-element.40.p0, bf16[80,1280]{1,0:T(8,128)(2,1)S(1)} %collective-permute-done.p1, ...), custom_call_target="tpu_custom_call" | custom-call | flops 1073741824 | bytes 4194304 | tf_op jit(solution)/shard_map/pallas_call | solution.py:232
  57.1 1.3 copy-done.8
  59.4 23.1 %all-to-all-done.1.landed_ref = bf16[64,48,256]{2,1,0:T(8,128)(2,1)S(1)} async-done(((bf16[64,48,256]{2,1,0:T(8,128)(2,1)}), bf16[64,48,256]{2,1,0:T(8,128)(2,1)S(1)}, u32[]{:S(2)}, u32[]{:S(2)}) %all-to-all-start.1) | async-done | bytes 1572896 | tf_op jit(solution)/shard_map/all_to_all | solution.py:364
  84.8 1.5 collective-permute-start.7
  86.3 5.6 %all-to-all-start = ((bf16[64,16,256]{2,1,0:T(8,128)(2,1)}), bf16[64,16,256]{2,1,0:T(8,128)(2,1)S(1)}, u32[]{:S(2)}, u32[]{:S(2)}) async-start(bf16[64,16,256]{2,1,0:T(8,128)(2,1)} %get-tuple-element.52), calls=%async_computation | async-start | bytes 1048576 | tf_op jit(solution)/shard_map/all_to_all | solution.py:364
  91.9 1.6 copy-done.9
  94.7 6.3 %shard_map.60 = (f32[2048,128]{1,0:T(8,128)S(1)}, f32[2048,256]{1,0:T(8,128)S(1)}) custom-call(f32[128,128]{1,0:T(8,128)S(1)} %get-tuple-element.50.flag_ref, bf16[2048,128]{1,0:T(8,128)(2,1)S(1)} %get-tuple-element.51.q_ref, f32[2048,128]{1,0:T(8,128)S(1)} %copy-done.11, f32[2048,256]{1,0:T(8,128)S(1)} %copy-done.9, bf16[1536,256]{1,0:T(8,128)(2,1)S(1)} %shard_map.59.refs_0_), custom_call_target="tpu_custom_call" | custom-call | flops 3221225472 | bytes 8388608 | tf_op jit(solution)/shard_map/pallas_call | solution.py:280
  101.0 2.6 %collective-permute-done.6.refs_0_ = bf16[1536,256]{1,0:T(8,128)(2,1)} collective-permute-done((bf16[1536,256]{1,0:T(8,128)(2,1)S(1)}, bf16[1536,256]{1,0:T(8,128)(2,1)}, u32[]{:S(2)}, u32[]{:S(2)}) %collective-permute-start.6) | collective-permute-done | bytes 786464 | tf_op jit(solution)/shard_map/ppermute | solution.py:317
  105.8 2.8 %collective-permute-start.9 = (bf16[768,256]{1,0:T(8,128)(2,1)S(1)}, bf16[768,256]{1,0:T(8,128)(2,1)S(1)}, u32[]{:S(2)}, u32[]{:S(2)}) collective-permute-start(bf16[768,256]{1,0:T(8,128)(2,1)S(1)} %slice.29), channel_id=1, source_target_pairs={{0,12},{4,0},{8,4},{12,8},{1,13},{5,1},{9,5},{13,9},{2,14},{6,2},{... | collective-permute-start | bytes 1179656 | tf_op jit(solution)/shard_map/ppermute | solution.py:317
  108.7 12.3 %shard_map.61 = (f32[2048,128]{1,0:T(8,128)S(1)}, f32[2048,256]{1,0:T(8,128)S(1)}) custom-call(f32[128,128]{1,0:T(8,128)S(1)} %get-tuple-element.50.flag_ref, bf16[2048,128]{1,0:T(8,128)(2,1)S(1)} %get-tuple-element.51.q_ref, f32[2048,128]{1,0:T(8,128)S(1)} %get-tuple-element.60.max_ref, f32[2048,256]{1,0:T(8,128)S(1)} %get-tuple-element.61.sum_ref, ...), custom_call_target="tpu_custom_call" | custom-call | flops 6442450944 | bytes 8388608 | tf_op jit(solution)/shard_map/pallas_call | solution.py:280
  122.1 8.0 %shard_map.62 = (f32[2048,128]{1,0:T(8,128)S(1)}, f32[2048,256]{1,0:T(8,128)S(1)}) custom-call(f32[128,128]{1,0:T(8,128)S(1)} %get-tuple-element.50.flag_ref, bf16[2048,128]{1,0:T(8,128)(2,1)S(1)} %copy-done.4, f32[2048,128]{1,0:T(8,128)S(1)} %get-tuple-element.62.max_ref, f32[2048,256]{1,0:T(8,128)S(1)} %get-tuple-element.63.sum_ref, ...), custom_call_target="tpu_custom_call" | custom-call | flops 3221225472 | bytes 8388608 | tf_op jit(solution)/shard_map/pallas_call | solution.py:280
  132.2 2.7 %collective-permute-start.11 = (bf16[512,256]{1,0:T(8,128)(2,1)S(1)}, bf16[512,256]{1,0:T(8,128)(2,1)S(1)}, u32[]{:S(2)}, u32[]{:S(2)}) collective-permute-start(bf16[512,256]{1,0:T(8,128)(2,1)S(1)} %shard_map.63.refs_0_), channel_id=1, source_target_pairs={{0,12},{4,0},{8,4},{12,8},{1,13},{5,1},{9,5},{13,9},{2,14},{6,2},{... | collective-permute-start | bytes 786440 | tf_op jit(solution)/shard_map/ppermute | solution.py:317
  134.8 6.1 %collective-permute-done.10.refs_0_ = bf16[512,256]{1,0:T(8,128)(2,1)S(1)} collective-permute-done((bf16[512,256]{1,0:T(8,128)(2,1)S(1)}, bf16[512,256]{1,0:T(8,128)(2,1)S(1)}, u32[]{:S(2)}, u32[]{:S(2)}) %collective-permute-start.10) | collective-permute-done | bytes 262176 | tf_op jit(solution)/shard_map/ppermute | solution.py:317
  141.1 2.7 %collective-permute-start.13 = (bf16[256,256]{1,0:T(8,128)(2,1)S(1)}, bf16[256,256]{1,0:T(8,128)(2,1)S(1)}, u32[]{:S(2)}, u32[]{:S(2)}) collective-permute-start(bf16[256,256]{1,0:T(8,128)(2,1)S(1)} %slice.31), channel_id=1, source_target_pairs={{0,12},{4,0},{8,4},{12,8},{1,13},{5,1},{9,5},{13,9},{2,14},{6,2},{... | collective-permute-start | bytes 393224 | tf_op jit(solution)/shard_map/ppermute | solution.py:317
  145.0 4.9 %shard_map.64 = (f32[2048,128]{1,0:T(8,128)S(1)}, f32[2048,256]{1,0:T(8,128)S(1)}) custom-call(f32[128,128]{1,0:T(8,128)S(1)} %get-tuple-element.50.flag_ref, bf16[2048,128]{1,0:T(8,128)(2,1)S(1)} %copy-done.5, f32[2048,128]{1,0:T(8,128)S(1)} %copy-done.2, f32[2048,256]{1,0:T(8,128)S(1)} %get-tuple-element.67.sum_ref, bf16[512,256]{1,0:T(8,128)(2,1)S(1)} %shard_map.63.refs_0_), custom_call_target="tpu_custom_call" | custom-call | flops 1073741824 | bytes 8388608 | tf_op jit(solution)/shard_map/pallas_call | solution.py:280
  149.9 7.6 %shard_map.65 = (bf16[64,1024]{1,0:T(8,128)(2,1)S(1)}, bf16[64,1024]{1,0:T(8,128)(2,1)S(1)}, bf16[64,1024]{1,0:T(8,128)(2,1)S(1)}, bf16[64,1024]{1,0:T(8,128)(2,1)S(1)}) custom-call(f32[128,128]{1,0:T(8,128)S(1)} %get-tuple-element.50.flag_ref, bf16[2048,128]{1,0:T(8,128)(2,1)S(1)} %copy-done.5, f32[2048,128]{1,0:T(8,128)S(1)} %get-tuple-element.69.max_ref, ...), custom_call_target="tpu_custom_call" | custom-call | flops 3221225472 | bytes 8388608 | tf_op jit(solution)/shard_map/pallas_call | solution.py:280
  157.6 1.8 %collective-permute-start.14 = (bf16[64,1024]{1,0:T(8,128)(2,1)S(1)}, bf16[64,1024]{1,0:T(8,128)(2,1)S(1)}, u32[]{:S(2)}, u32[]{:S(2)}) collective-permute-start(bf16[64,1024]{1,0:T(8,128)(2,1)S(1)} %get-tuple-element.72), channel_id=1, source_target_pairs={{0,1},{1,0},{2,3},{3,2},{4,5},{5,4},{6,7},{7,6},{8,9},{9,8},{10,11... | collective-permute-start | bytes 393224 | tf_op jit(solution)/shard_map/ppermute | solution.py:312
  159.3 2.7 %collective-permute-start.15 = (bf16[64,1024]{1,0:T(8,128)(2,1)S(1)}, bf16[64,1024]{1,0:T(8,128)(2,1)S(1)}, u32[]{:S(2)}, u32[]{:S(2)}) collective-permute-start(bf16[64,1024]{1,0:T(8,128)(2,1)S(1)} %get-tuple-element.73), channel_id=1, source_target_pairs={{0,2},{1,3},{2,0},{3,1},{4,6},{5,7},{6,4},{7,5},{8,10},{9,11},{10,... | collective-permute-start | bytes 393224 | tf_op jit(solution)/shard_map/ppermute | solution.py:312
  162.1 2.9 %collective-permute-start.16 = (bf16[64,1024]{1,0:T(8,128)(2,1)S(1)}, bf16[64,1024]{1,0:T(8,128)(2,1)S(1)}, u32[]{:S(2)}, u32[]{:S(2)}) collective-permute-start(bf16[64,1024]{1,0:T(8,128)(2,1)S(1)} %get-tuple-element.74), channel_id=1, source_target_pairs={{0,3},{1,2},{2,1},{3,0},{4,7},{5,6},{6,5},{7,4},{8,11},{9,10},{10,... | collective-permute-start | bytes 393224 | tf_op jit(solution)/shard_map/ppermute | solution.py:312
  165.0 5.1 %collective-permute-done.15.refs_2_ = bf16[64,1024]{1,0:T(8,128)(2,1)S(1)} collective-permute-done((bf16[64,1024]{1,0:T(8,128)(2,1)S(1)}, bf16[64,1024]{1,0:T(8,128)(2,1)S(1)}, u32[]{:S(2)}, u32[]{:S(2)}) %collective-permute-start.15) | collective-permute-done | bytes 131104 | tf_op jit(solution)/shard_map/ppermute | solution.py:312
  170.1 5.0 %collective-permute-done.16.refs_3_ = bf16[64,1024]{1,0:T(8,128)(2,1)S(1)} collective-permute-done((bf16[64,1024]{1,0:T(8,128)(2,1)S(1)}, bf16[64,1024]{1,0:T(8,128)(2,1)S(1)}, u32[]{:S(2)}, u32[]{:S(2)}) %collective-permute-start.16) | collective-permute-done | bytes 131104 | tf_op jit(solution)/shard_map/ppermute | solution.py:312
  (60 shorter events, 19.1 us)
Async XLA Ops:
  2.8 1.0 copy-start.6
  3.8 0.9 copy-start.7
  4.8 12.5 %collective-permute-start = (bf16[80,1280]{1,0:T(8,128)(2,1)S(1)}, bf16[80,1280]{1,0:T(8,128)(2,1)S(1)}, u32[]{:S(2)}, u32[]{:S(2)}) collective-permute-start(bf16[80,1280]{1,0:T(8,128)(2,1)S(1)} %get-tuple-element.43), channel_id=1, source_target_pairs={{0,1},{1,0},{2,3},{3,2},{4,5},{5,4},{6,7},{7,6},{8,9},{9,8},{10,11... | collective-permute-start | bytes 614408 | tf_op jit(solution)/shard_map/ppermute | solution.py:312
  8.1 10.5 %collective-permute-start.1 = (bf16[80,1280]{1,0:T(8,128)(2,1)S(1)}, bf16[80,1280]{1,0:T(8,128)(2,1)S(1)}, u32[]{:S(2)}, u32[]{:S(2)}) collective-permute-start(bf16[80,1280]{1,0:T(8,128)(2,1)S(1)} %get-tuple-element.44), channel_id=1, source_target_pairs={{0,2},{1,3},{2,0},{3,1},{4,6},{5,7},{6,4},{7,5},{8,10},{9,11},{10,... | collective-permute-start | bytes 614408 | tf_op jit(solution)/shard_map/ppermute | solution.py:312
  13.3 12.2 %collective-permute-start.2 = (bf16[80,1280]{1,0:T(8,128)(2,1)S(1)}, bf16[80,1280]{1,0:T(8,128)(2,1)S(1)}, u32[]{:S(2)}, u32[]{:S(2)}) collective-permute-start(bf16[80,1280]{1,0:T(8,128)(2,1)S(1)} %get-tuple-element.45), channel_id=1, source_target_pairs={{0,3},{1,2},{2,1},{3,0},{4,7},{5,6},{6,5},{7,4},{8,11},{9,10},{10,... | collective-permute-start | bytes 614408 | tf_op jit(solution)/shard_map/ppermute | solution.py:312
  13.8 1.2 copy-start
  25.6 57.0 %all-to-all-start.1 = ((bf16[64,48,256]{2,1,0:T(8,128)(2,1)}), bf16[64,48,256]{2,1,0:T(8,128)(2,1)S(1)}, u32[]{:S(2)}, u32[]{:S(2)}) async-start(bf16[64,48,256]{2,1,0:T(8,128)(2,1)} %get-tuple-element.53), calls=%async_computation.1 | async-start | bytes 3145728 | tf_op jit(solution)/shard_map/all_to_all | solution.py:364
  41.8 6.6 %collective-permute-start.3 = (bf16[320,256]{1,0:T(8,128)(2,1)S(1)}, bf16[320,256]{1,0:T(8,128)(2,1)S(1)}, u32[]{:S(2)}, u32[]{:S(2)}) collective-permute-start(bf16[320,256]{1,0:T(8,128)(2,1)S(1)} %get-tuple-element.49), channel_id=1, source_target_pairs={{0,4},{4,8},{8,12},{12,0},{1,5},{5,9},{9,13},{13,1},{2,6},{6,10},{... | collective-permute-start | bytes 491528 | tf_op jit(solution)/shard_map/ppermute | solution.py:317
  43.1 5.3 %collective-permute-start.4 = (bf16[320,256]{1,0:T(8,128)(2,1)S(1)}, bf16[320,256]{1,0:T(8,128)(2,1)S(1)}, u32[]{:S(2)}, u32[]{:S(2)}) collective-permute-start(bf16[320,256]{1,0:T(8,128)(2,1)S(1)} %get-tuple-element.49), channel_id=1, source_target_pairs={{0,12},{4,0},{8,4},{12,8},{1,13},{5,1},{9,5},{13,9},{2,14},{6,2},{... | collective-permute-start | bytes 491528 | tf_op jit(solution)/shard_map/ppermute | solution.py:317
  44.6 8.3 %collective-permute-start.5 = (bf16[320,256]{1,0:T(8,128)(2,1)S(1)}, bf16[320,256]{1,0:T(8,128)(2,1)S(1)}, u32[]{:S(2)}, u32[]{:S(2)}) collective-permute-start(bf16[320,256]{1,0:T(8,128)(2,1)S(1)} %get-tuple-element.49), channel_id=1, source_target_pairs={{0,8},{4,12},{8,0},{12,4},{1,9},{5,13},{9,1},{13,5},{2,10},{6,14},... | collective-permute-start | bytes 491528 | tf_op jit(solution)/shard_map/ppermute | solution.py:317
  57.1 1.3 copy-start.8
  58.4 1.0 copy-start.10
  59.4 49.3 %copy-start.3 = (bf16[2048,128]{1,0:T(8,128)(2,1)}, bf16[2048,128]{1,0:T(8,128)(2,1)S(1)}, u32[]{:S(2)}) copy-start(bf16[2048,128]{1,0:T(8,128)(2,1)S(1)} %get-tuple-element.51.q_ref) | copy-start | bytes 1572868
  83.5 20.1 %collective-permute-start.6 = (bf16[1536,256]{1,0:T(8,128)(2,1)S(1)}, bf16[1536,256]{1,0:T(8,128)(2,1)}, u32[]{:S(2)}, u32[]{:S(2)}) collective-permute-start(bf16[1536,256]{1,0:T(8,128)(2,1)S(1)} %shard_map.59.refs_0_), channel_id=1, source_target_pairs={{0,4},{4,8},{8,12},{12,0},{1,5},{5,9},{9,13},{13,1},{2,6},{6,10},{... | collective-permute-start | bytes 2359304 | tf_op jit(solution)/shard_map/ppermute | solution.py:317
  84.8 20.0 %collective-permute-start.7 = (bf16[1536,256]{1,0:T(8,128)(2,1)S(1)}, bf16[1536,256]{1,0:T(8,128)(2,1)}, u32[]{:S(2)}, u32[]{:S(2)}) collective-permute-start(bf16[1536,256]{1,0:T(8,128)(2,1)S(1)} %shard_map.59.refs_0_), channel_id=1, source_target_pairs={{0,12},{4,0},{8,4},{12,8},{1,13},{5,1},{9,5},{13,9},{2,14},{6,2},{... | collective-permute-start | bytes 2359304 | tf_op jit(solution)/shard_map/ppermute | solution.py:317
  86.3 44.8 %all-to-all-start = ((bf16[64,16,256]{2,1,0:T(8,128)(2,1)}), bf16[64,16,256]{2,1,0:T(8,128)(2,1)S(1)}, u32[]{:S(2)}, u32[]{:S(2)}) async-start(bf16[64,16,256]{2,1,0:T(8,128)(2,1)} %get-tuple-element.52), calls=%async_computation | async-start | bytes 1048576 | tf_op jit(solution)/shard_map/all_to_all | solution.py:364
  91.8 1.6 copy-start.9
  93.4 1.2 copy-start.11
  104.6 16.4 %collective-permute-start.8 = (bf16[768,256]{1,0:T(8,128)(2,1)S(1)}, bf16[768,256]{1,0:T(8,128)(2,1)S(1)}, u32[]{:S(2)}, u32[]{:S(2)}) collective-permute-start(bf16[768,256]{1,0:T(8,128)(2,1)S(1)} %slice.28), channel_id=1, source_target_pairs={{0,4},{4,8},{8,12},{12,0},{1,5},{5,9},{9,13},{13,1},{2,6},{6,10},{... | collective-permute-start | bytes 1179656 | tf_op jit(solution)/shard_map/ppermute | solution.py:317
  105.8 15.2 %collective-permute-start.9 = (bf16[768,256]{1,0:T(8,128)(2,1)S(1)}, bf16[768,256]{1,0:T(8,128)(2,1)S(1)}, u32[]{:S(2)}, u32[]{:S(2)}) collective-permute-start(bf16[768,256]{1,0:T(8,128)(2,1)S(1)} %slice.29), channel_id=1, source_target_pairs={{0,12},{4,0},{8,4},{12,8},{1,13},{5,1},{9,5},{13,9},{2,14},{6,2},{... | collective-permute-start | bytes 1179656 | tf_op jit(solution)/shard_map/ppermute | solution.py:317
  121.0 1.0 copy-start.4
  122.1 21.7 %copy-start.5 = (bf16[2048,128]{1,0:T(8,128)(2,1)S(1)}, bf16[2048,128]{1,0:T(8,128)(2,1)}, u32[]{:S(2)}) copy-start(bf16[2048,128]{1,0:T(8,128)(2,1)} %copy-done.3) | copy-start | bytes 1572868
  130.1 1.0 copy-start.1
  132.1 8.9 %collective-permute-start.10 = (bf16[512,256]{1,0:T(8,128)(2,1)S(1)}, bf16[512,256]{1,0:T(8,128)(2,1)S(1)}, u32[]{:S(2)}, u32[]{:S(2)}) collective-permute-start(bf16[512,256]{1,0:T(8,128)(2,1)S(1)} %shard_map.63.refs_0_), channel_id=1, source_target_pairs={{0,4},{4,8},{8,12},{12,0},{1,5},{5,9},{9,13},{13,1},{2,6},{6,10},{... | collective-permute-start | bytes 786440 | tf_op jit(solution)/shard_map/ppermute | solution.py:317
  132.2 8.9 %collective-permute-start.11 = (bf16[512,256]{1,0:T(8,128)(2,1)S(1)}, bf16[512,256]{1,0:T(8,128)(2,1)S(1)}, u32[]{:S(2)}, u32[]{:S(2)}) collective-permute-start(bf16[512,256]{1,0:T(8,128)(2,1)S(1)} %shard_map.63.refs_0_), channel_id=1, source_target_pairs={{0,12},{4,0},{8,4},{12,8},{1,13},{5,1},{9,5},{13,9},{2,14},{6,2},{... | collective-permute-start | bytes 786440 | tf_op jit(solution)/shard_map/ppermute | solution.py:317
  140.9 9.0 %collective-permute-start.12 = (bf16[256,256]{1,0:T(8,128)(2,1)S(1)}, bf16[256,256]{1,0:T(8,128)(2,1)S(1)}, u32[]{:S(2)}, u32[]{:S(2)}) collective-permute-start(bf16[256,256]{1,0:T(8,128)(2,1)S(1)} %slice.30), channel_id=1, source_target_pairs={{0,4},{4,8},{8,12},{12,0},{1,5},{5,9},{9,13},{13,1},{2,6},{6,10},{... | collective-permute-start | bytes 393224 | tf_op jit(solution)/shard_map/ppermute | solution.py:317
  141.1 8.8 %collective-permute-start.13 = (bf16[256,256]{1,0:T(8,128)(2,1)S(1)}, bf16[256,256]{1,0:T(8,128)(2,1)S(1)}, u32[]{:S(2)}, u32[]{:S(2)}) collective-permute-start(bf16[256,256]{1,0:T(8,128)(2,1)S(1)} %slice.31), channel_id=1, source_target_pairs={{0,12},{4,0},{8,4},{12,8},{1,13},{5,1},{9,5},{13,9},{2,14},{6,2},{... | collective-permute-start | bytes 393224 | tf_op jit(solution)/shard_map/ppermute | solution.py:317
  143.8 1.2 copy-start.2
  157.6 7.4 %collective-permute-start.14 = (bf16[64,1024]{1,0:T(8,128)(2,1)S(1)}, bf16[64,1024]{1,0:T(8,128)(2,1)S(1)}, u32[]{:S(2)}, u32[]{:S(2)}) collective-permute-start(bf16[64,1024]{1,0:T(8,128)(2,1)S(1)} %get-tuple-element.72), channel_id=1, source_target_pairs={{0,1},{1,0},{2,3},{3,2},{4,5},{5,4},{6,7},{7,6},{8,9},{9,8},{10,11... | collective-permute-start | bytes 393224 | tf_op jit(solution)/shard_map/ppermute | solution.py:312
  159.3 10.7 %collective-permute-start.15 = (bf16[64,1024]{1,0:T(8,128)(2,1)S(1)}, bf16[64,1024]{1,0:T(8,128)(2,1)S(1)}, u32[]{:S(2)}, u32[]{:S(2)}) collective-permute-start(bf16[64,1024]{1,0:T(8,128)(2,1)S(1)} %get-tuple-element.73), channel_id=1, source_target_pairs={{0,2},{1,3},{2,0},{3,1},{4,6},{5,7},{6,4},{7,5},{8,10},{9,11},{10,... | collective-permute-start | bytes 393224 | tf_op jit(solution)/shard_map/ppermute | solution.py:312
  162.1 13.0 %collective-permute-start.16 = (bf16[64,1024]{1,0:T(8,128)(2,1)S(1)}, bf16[64,1024]{1,0:T(8,128)(2,1)S(1)}, u32[]{:S(2)}, u32[]{:S(2)}) collective-permute-start(bf16[64,1024]{1,0:T(8,128)(2,1)S(1)} %get-tuple-element.74), channel_id=1, source_target_pairs={{0,3},{1,2},{2,1},{3,0},{4,7},{5,6},{6,5},{7,4},{8,11},{9,10},{10,... | collective-permute-start | bytes 393224 | tf_op jit(solution)/shard_map/ppermute | solution.py:312

commit v2 on v1

v2 whole, which is shorter than its diff:
```python
import functools
import math

import jax
import jax.numpy as jnp
from jax import lax
from jax.experimental import pallas as pl
from jax.experimental.pallas import tpu as pltpu
from jax.sharding import Mesh, PartitionSpec as P

HQ = 32
KVH = 4
HD = 128
GROUP_HEADS = HQ // KVH
BLK = 64
GROUPS = 16
LOCAL = 8
STORED = 8
ROWS = 64
INFO_ROWS = 16
QCOLS = GROUP_HEADS * HD
PIECE = QCOLS + 3 * HD
HEAD_ROWS = 4 * ROWS
ALL_ROWS = GROUP_HEADS * HEAD_ROWS
UNROLL = 4
EXP2_SCALE = math.log2(math.e) / math.sqrt(HD)
LOWEST = -1e30
CHUNKS = (48, 16)
KEY_TILE = 1024

AXES = ("zlo", "y", "x", "zhi", "core")
HEAD_AXES = ("zhi", "core")
SEND_AXES = ("zlo", "y", "zhi", "core")

VMEM = pl.BlockSpec(memory_space=pltpu.VMEM)
SMEM = pl.BlockSpec(memory_space=pltpu.SMEM)
BF16 = jnp.bfloat16


def params(mib=24):
    return pltpu.CompilerParams(vmem_limit_bytes=mib * 2**20)


def cost(flops, size):
    return pl.CostEstimate(flops=flops, bytes_accessed=size, transcendentals=0)


def bf16_shape(*dims):
    return jax.ShapeDtypeStruct(dims, BF16)


def columns(index, width):
    return pl.ds(pl.multiple_of(index * width, width), width)


def split_kernel(place_ref, q_ref, kv_ref, wanted_ref, live_ref, *refs):
    outs, info = refs[:4], refs[4]
    mine = pl.ds(place_ref[1], 1)
    owners = (wanted_ref[mine, :] // (GROUPS * STORED)).astype(jnp.float32)
    info[...] = jnp.broadcast_to(live_ref[mine, :].astype(jnp.float32), (ROWS, HD))
    info[:, :LOCAL] = jnp.broadcast_to(owners, (ROWS, LOCAL))
    for offset, out in enumerate(outs):
        head = place_ref[0] ^ offset
        out[:, :QCOLS] = q_ref[:, columns(head, QCOLS)]
        out[:, QCOLS : QCOLS + HD] = kv_ref[:, columns(head, HD)]
        out[:, QCOLS + HD : QCOLS + 2 * HD] = kv_ref[:, columns(KVH + head, HD)]
        out[:, QCOLS + 2 * HD :] = info[...].astype(BF16)


def split_queries(place, queries, question_kv, wanted, live):
    return pl.pallas_call(
        split_kernel,
        out_shape=[bf16_shape(ROWS, PIECE)] * 4,
        in_specs=[SMEM] + [VMEM] * 4,
        out_specs=[VMEM] * 4,
        scratch_shapes=[pltpu.VMEM((ROWS, HD), jnp.float32)],
        compiler_params=params(16),
        cost_estimate=cost(0, 1 << 20),
    )(place, queries, question_kv, wanted, live)


def select_kernel(slot_ref, stored_ref, *outs):
    def one(group, carry):
        slot = slot_ref[group]
        start = 0
        for size, out in zip(CHUNKS, outs):
            tokens = slice(start, start + size)
            for head in range(KVH):
                keys = slice(head * HD, (head + 1) * HD)
                values = slice((KVH + head) * HD, (KVH + head + 1) * HD)
                out[group * KVH + head, :, :HD] = stored_ref[slot, tokens, keys]
                out[group * KVH + head, :, HD:] = stored_ref[slot, tokens, values]
            start += size
        return carry

    lax.fori_loop(0, GROUPS, one, 0)


def select_blocks(slots, stored):
    return pl.pallas_call(
        select_kernel,
        out_shape=[bf16_shape(GROUPS * KVH, size, 2 * HD) for size in CHUNKS],
        in_specs=[SMEM, VMEM],
        out_specs=[VMEM] * len(CHUNKS),
        compiler_params=params(16),
        cost_estimate=cost(0, 3 << 20),
    )(slots, stored)


def collect_kernel(p0, p1, p2, p3, question, info):
    for offset, piece in enumerate((p0, p1, p2, p3)):
        question[offset * ROWS : (offset + 1) * ROWS, :] = piece[:, QCOLS:]
        told = piece[:INFO_ROWS, QCOLS + 2 * HD :].astype(jnp.float32)
        info[offset : offset + 1, :] = told[:1, :].astype(jnp.int32)


def collect(pieces):
    return pl.pallas_call(
        collect_kernel,
        out_shape=[bf16_shape(HEAD_ROWS, 3 * HD), jax.ShapeDtypeStruct((4, HD), jnp.int32)],
        in_specs=[VMEM] * 4,
        out_specs=[VMEM] * 2,
        compiler_params=params(16),
        cost_estimate=cost(0, 1 << 20),
    )(*pieces)


def pack_kernel(slot_ref, flag_ref, landed_ref, token_ref, out_ref):
    tokens = landed_ref.shape[1]

    def one(entry, carry):
        rows = columns(entry, tokens)
        out_ref[rows, :] = landed_ref[slot_ref[entry]]

        @pl.when(flag_ref[entry] == 0)
        def _():
            out_ref[rows, HD:] = jnp.zeros((tokens, HD), BF16)

        return carry

    lax.fori_loop(0, 4 * LOCAL, one, 0)


def pack_blocks(slots, flags, landed, token):
    tokens = landed.shape[1]
    return pl.pallas_call(
        pack_kernel,
        out_shape=bf16_shape(4 * LOCAL * tokens, 2 * HD),
        in_specs=[SMEM, SMEM, VMEM, VMEM],
        out_specs=VMEM,
        compiler_params=params(16),
        cost_estimate=cost(0, 3 << 20),
    )(slots, flags, landed, token)


def step(query, keys, values, state_max, state_sum, mask=None):
    scores = lax.dot_general(
        query, keys, (((1,), (1,)), ((), ())), preferred_element_type=jnp.float32
    )
    if mask is not None:
        scores = jnp.where(mask, scores, LOWEST)
    new_max = jnp.maximum(state_max, jnp.max(scores, axis=1, keepdims=True))
    scale = jnp.exp2((state_max - new_max) * EXP2_SCALE)
    weights = jnp.exp2((scores - new_max[:, :1]) * EXP2_SCALE).astype(jnp.bfloat16)
    summed = jnp.dot(weights, values, preferred_element_type=jnp.float32)
    return new_max, state_sum * jnp.concatenate([scale, scale], axis=1) + summed


TOKEN = jax.ShapeDtypeStruct((8, HD), jnp.float32)


def question_kernel(place_ref, p0, p1, p2, p3, left, right, far, *refs):
    q_out, max_out, sum_out, flag_out, token, held = refs
    head, column = place_ref[0], place_ref[1]
    token[...] = jnp.zeros(TOKEN.shape, jnp.float32)
    ones = jnp.ones((HEAD_ROWS, HD), BF16)
    entry = lax.broadcasted_iota(jnp.int32, (LOCAL, HD), 0).astype(jnp.float32)

    def hold(slot, offset, piece, row, start):
        held[slot, offset * ROWS : (offset + 1) * ROWS, :] = piece[
            row : row + ROWS, start : start + 2 * HD
        ]
        info = piece[row : row + INFO_ROWS, start + 2 * HD :].astype(jnp.float32)
        count = jnp.broadcast_to(info[:1, LOCAL : LOCAL + 1], (LOCAL, HD))
        first = (slot * 4 + offset) * LOCAL
        flag_out[first : first + LOCAL, :] = (entry < count).astype(jnp.float32)

    for offset, piece in enumerate((p0, p1, p2, p3)):
        hold(0, offset, piece, 0, QCOLS)
        for h in range(GROUP_HEADS):
            start = h * HEAD_ROWS + offset * ROWS
            q_out[start : start + ROWS, :] = piece[:, h * HD : (h + 1) * HD]
        for slot, other in enumerate((left, right, far)):
            hold(slot + 1, offset, other, offset * ROWS, 0)

    def positions(axis, shape):
        index = lax.broadcasted_iota(jnp.int32, shape, axis)
        return ((index // ROWS) ^ head) * ROWS + index % ROWS

    shape = (HEAD_ROWS, HEAD_ROWS)
    mask = positions(1, shape) <= positions(0, shape)
    low = jnp.full((HEAD_ROWS, HD), LOWEST, jnp.float32)
    zero = jnp.zeros((HEAD_ROWS, 2 * HD), jnp.float32)

    def first(h, carry):
        rows = columns(h, HEAD_ROWS)
        values = jnp.concatenate([held[0, :, HD:], ones], axis=1)
        max_out[rows, :], sum_out[rows, :] = step(
            q_out[rows, :], held[0, :, :HD], values, low, zero, mask
        )
        return carry

    lax.fori_loop(0, GROUP_HEADS, first, 0, unroll=2)
    for least, slot in ((1, 1), (2, 3), (3, 2)):

        @pl.when(column >= least)
        def _(slot=slot):
            def more(h, carry):
                rows = columns(h, HEAD_ROWS)
                values = jnp.concatenate([held[slot, :, HD:], ones], axis=1)
                max_out[rows, :], sum_out[rows, :] = step(
                    q_out[rows, :], held[slot, :, :HD], values, max_out[rows, :], sum_out[rows, :]
                )
                return carry

            lax.fori_loop(0, GROUP_HEADS, more, 0, unroll=2)


STATE = (
    jax.ShapeDtypeStruct((ALL_ROWS, HD), jnp.float32),
    jax.ShapeDtypeStruct((ALL_ROWS, 2 * HD), jnp.float32),
)


def question_part(place, pieces, left, right, far):
    flags = jax.ShapeDtypeStruct((16 * LOCAL, HD), jnp.float32)
    return pl.pallas_call(
        question_kernel,
        out_shape=[bf16_shape(ALL_ROWS, HD), *STATE, flags, TOKEN],
        in_specs=[SMEM] + [VMEM] * 7,
        out_specs=[VMEM] * 5,
        scratch_shapes=[pltpu.VMEM((4, HEAD_ROWS, 2 * HD), BF16)],
        compiler_params=params(),
        cost_estimate=cost(4 * ALL_ROWS * 1024 * HD, 4 << 20),
    )(place, *pieces, left, right, far)


def halves_kernel(left_ref, right_ref, token_ref, left_out, right_out):
    middle = left_out.shape[0]
    left_out[...] = left_ref[:middle, :]
    right_out[...] = right_ref[middle:, :]


def halves(left, right, token):
    return pl.pallas_call(
        halves_kernel,
        out_shape=[bf16_shape(left.shape[0] // 2, 2 * HD)] * 2,
        in_specs=[VMEM] * 3,
        out_specs=[VMEM] * 2,
        compiler_params=params(16),
        cost_estimate=cost(0, 1 << 20),
    )(left, right, token)


def passage_kernel(layout, last, flag_ref, q_ref, max_in, sum_in, *refs):
    tiles, refs = refs[: len(layout)], refs[len(layout) :]
    outs, (key_ref, value_ref) = refs[:-2], refs[-2:]
    if not last:
        outs[2][...] = jnp.zeros(TOKEN.shape, jnp.float32)
    start = 0
    for (first, blocks), tile in zip(layout, tiles):
        size = tile.shape[0]
        tokens = size // blocks
        key_ref[start : start + size, :] = tile[:, :HD]
        value_ref[start : start + size, :HD] = tile[:, HD:]
        for block in range(blocks):
            flag = jnp.broadcast_to(flag_ref[first + block : first + block + 1, :], (tokens, HD))
            rows = slice(start + block * tokens, start + (block + 1) * tokens)
            value_ref[rows, HD:] = flag.astype(BF16)
        start += size
    total = start
    parts = -(-total // KEY_TILE)
    width = total // parts

    def one(h, carry):
        rows = columns(h, HEAD_ROWS)
        query, state_max, state_sum = q_ref[rows, :], max_in[rows, :], sum_in[rows, :]
        for part in range(parts):
            keys = slice(part * width, (part + 1) * width)
            state_max, state_sum = step(
                query, key_ref[keys, :], value_ref[keys, :], state_max, state_sum
            )
        if last:
            result = (state_sum[:, :HD] / state_sum[:, HD:]).astype(BF16)
            for offset, out in enumerate(outs):
                out[:, columns(h, HD)] = result[offset * ROWS : (offset + 1) * ROWS, :]
        else:
            outs[0][rows, :] = state_max
            outs[1][rows, :] = state_sum
        return carry

    lax.fori_loop(0, GROUP_HEADS, one, 0, unroll=UNROLL)


def passage_part(flags, query, state, tiles, layout, last):
    shapes = [bf16_shape(ROWS, QCOLS)] * 4 if last else [*STATE, TOKEN]
    keys = sum(tile.shape[0] for tile in tiles)
    return pl.pallas_call(
        functools.partial(passage_kernel, layout, last),
        out_shape=shapes,
        in_specs=[VMEM] * (4 + len(tiles)),
        out_specs=[VMEM] * len(shapes),
        scratch_shapes=[
            pltpu.VMEM((keys, HD), BF16),
            pltpu.VMEM((keys, 2 * HD), BF16),
        ],
        compiler_params=params(),
        cost_estimate=cost(4 * ALL_ROWS * keys * HD * 2, 8 << 20),
    )(flags, query, *state, *tiles)


def join_kernel(head_ref, *refs):
    out = refs[-1]
    for offset, piece in enumerate(refs[:-1]):
        out[:, columns(head_ref[0] ^ offset, QCOLS)] = piece[...]


def join_outputs(head, pieces):
    return pl.pallas_call(
        join_kernel,
        out_shape=bf16_shape(ROWS, HQ * HD),
        in_specs=[SMEM] + [VMEM] * 4,
        out_specs=VMEM,
        compiler_params=params(16),
        cost_estimate=cost(0, 1 << 20),
    )(head, *pieces)


def swap_heads(pieces):
    moved = [pieces[0]]
    for offset in range(1, 4):
        pairs = [(i, i ^ offset) for i in range(4)]
        moved.append(lax.ppermute(pieces[offset], HEAD_AXES, pairs))
    return moved


def along(axis, value, hops):
    return lax.ppermute(value, axis, [(i, (i + hops) % 4) for i in range(4)])


def ints(*values):
    return jnp.stack([jnp.asarray(value, jnp.int32) for value in values])


def body(queries, question_kv, passage_kv, wanted, live):
    x = lax.axis_index("x")
    store = lax.axis_index("zlo") * 4 + lax.axis_index("y")
    head = lax.axis_index("zhi") * 2 + lax.axis_index("core")

    wanted_ids = wanted[:, 0, :]
    owner_ids = wanted_ids // (GROUPS * STORED)
    slots = jnp.sum(jnp.where(owner_ids == store, wanted_ids % STORED, 0), axis=1)
    slots = slots.astype(jnp.int32)

    split = split_queries(ints(head, store), queries, question_kv, wanted_ids, live)
    pieces = swap_heads(split)
    outgoing = select_blocks(slots, passage_kv)
    *outgoing, p1, p2, p3 = lax.optimization_barrier((*outgoing, *pieces[1:]))
    pieces = [pieces[0], p1, p2, p3]

    question, near = collect(pieces)
    owners, counts = near[:, :LOCAL], near[:, LOCAL : LOCAL + 1]
    offset = lax.broadcasted_iota(jnp.int32, (4, LOCAL), 0)
    slot = owners * KVH + (head ^ offset)
    read = lax.broadcasted_iota(jnp.int32, (4, LOCAL), 1) < counts
    landed_slots = jnp.where(read, slot, slot[:, :1]).reshape(-1)
    landed_flags = read.astype(jnp.int32).reshape(-1)

    query, *state, flags, token = question_part(
        ints(head, x),
        pieces,
        along("x", question, 1),
        along("x", question, 3),
        along("x", question, 2),
    )

    quarter, half = 4 * LOCAL, 2 * LOCAL
    own_flags, left_flags, right_flags = [(i * quarter, quarter) for i in range(3)]
    far_flags = ((3 * quarter, half), (3 * quarter + half, half))

    def fetch(chunk, token):
        landed = lax.all_to_all(outgoing[chunk], SEND_AXES, 0, 0, tiled=True)
        own = pack_blocks(landed_slots, landed_flags, landed, token)
        return own, along("x", own, 1), along("x", own, 3)

    def relay(left, right, token):
        first, second = halves(left, right, token)
        return along("x", first, 1), along("x", second, 3)

    attend = functools.partial(passage_part, flags, query)
    own, left, right = fetch(0, token)
    *state, token = attend(state, (own,), (own_flags,), False)
    far = relay(left, right, token)
    *state, token = attend(state, (left, right), (left_flags, right_flags), False)
    own, left, right = fetch(1, token)
    *state, token = attend(state, far, far_flags, False)
    far = relay(left, right, token)
    layout = (own_flags, left_flags, right_flags)
    *state, token = attend(state, (own, left, right), layout, False)
    state = attend(state, far, far_flags, True)

    return join_outputs(ints(head), swap_heads(state))


def solution(mesh):
    fine = Mesh(mesh.devices.reshape(4, 4, 4, 2, 2), AXES)
    store, ctx = ("zlo", "y"), ("x", "zhi", "core")
    every = store + ctx
    return jax.shard_map(
        body,
        mesh=fine,
        in_specs=(
            P(every, None),
            P(every, None),
            P(every, None, None),
            P(None, ctx, None),
            P(None, ctx),
        ),
        out_specs=P(every, None),
        check_vma=False,
    )
```

time: 177 us -> 161 us (0.910)
  Pallas kernels: 48.5 us -> 38.1 us
  starting transfers between devices: 53.7 us -> 49.6 us
  local copies, waits for them, and re-layouts: 14 us -> 16.2 us
  other arithmetic: 3.08 us -> 1.08 us
    pallas_call x5, Pallas kernels: 39.2 us -> 28.8 us  [passage_part(): pl.pallas_call(functools.partial(passage_kernel, layout, last), out_shape...]
    unnamed x24 -> x25, local copies, waits for them, and re-layouts: 11.5 us -> 14.9 us
    all_to_all x2, starting transfers between devices: 21.7 us -> 19.4 us  [fetch(): landed = lax.all_to_all(outgoing[chunk], SEND_AXES, 0, 0, tiled=True)]
    slice x5 -> x1, local copies, waits for them, and re-layouts: 2.18 us -> 0.18 us  [body(): owners, counts = (near[:, :LOCAL], near[:, LOCAL:LOCAL + 1])]
    ppermute x11, starting transfers between devices: 15.6 us -> 13.8 us  [along(): return lax.ppermute(value, axis, [(i, (i + hops) % 4) for i in range(4)])]
  transfers between devices with their start and end apart: 19 -> 19, of which waited for: 9 -> 8; matrix products, arithmetic and copies ran while one was open for 2% -> 1% of each run, Pallas kernels for 22% -> 20%
where the time goes in v2:
time: 161 us; the launch traced here: 160 us
  waiting for transfers between devices  55.3 us (34%)
  starting transfers between devices  49.6 us (31%)
  Pallas kernels  38.1 us (24%)
  local copies, waits for them, and re-layouts  16.2 us (10%)
    pallas_call x5, Pallas kernels, passage_part(): pl.pallas_call(functools.partial(passage_kernel, layout, last), out_shape...  28.8 us
    all_to_all x2, waiting for transfers between devices, fetch(): landed = lax.all_to_all(outgoing[chunk], SEND_AXES, 0, 0, tiled=True)  23.7 us
    all_to_all x2, starting transfers between devices, fetch(): landed = lax.all_to_all(outgoing[chunk], SEND_AXES, 0, 0, tiled=True)  19.4 us
    ppermute x6, waiting for transfers between devices, swap_heads(): moved.append(lax.ppermute(pieces[offset], HEAD_AXES, pairs))  17.7 us
    ppermute x6, starting transfers between devices, swap_heads(): moved.append(lax.ppermute(pieces[offset], HEAD_AXES, pairs))  16.4 us
    unnamed x25, local copies, waits for them, and re-layouts  14.9 us
    ppermute x11, waiting for transfers between devices, along(): return lax.ppermute(value, axis, [(i, (i + hops) % 4) for i in range(4)])  13.9 us
    ppermute x11, starting transfers between devices, along(): return lax.ppermute(value, axis, [(i, (i + hops) % 4) for i in range(4)])  13.8 us
  transfers between devices with their start and end apart: 19, of which 8 were waited for; matrix products, arithmetic and copies ran while one was open for 1% of the time, Pallas kernels for 20%

profile of v2, /device:TPU:1, one launch (start us, length us, event | category | flops | bytes accessed | tf_op | source)
XLA Modules:
  0.0 160.4 jit_solution(16874589042955637922)
XLA Ops:
  4.1 3.3 %collective-permute-start = (bf16[64,1408]{1,0:T(8,128)(2,1)S(1)}, bf16[64,1408]{1,0:T(8,128)(2,1)S(1)}, u32[]{:S(2)}, u32[]{:S(2)}) collective-permute-start(bf16[64,1408]{1,0:T(8,128)(2,1)S(1)} %get-tuple-element.45), channel_id=1, source_target_pairs={{0,1},{1,0},{2,3},{3,2},{4,5},{5,4},{6,7},{7,6},{8,9},{9,8},{10,11... | collective-permute-start | bytes 540680 | tf_op jit(solution)/shard_map/ppermute | solution.py:343
  7.5 5.2 %collective-permute-start.1 = (bf16[64,1408]{1,0:T(8,128)(2,1)S(1)}, bf16[64,1408]{1,0:T(8,128)(2,1)S(1)}, u32[]{:S(2)}, u32[]{:S(2)}) collective-permute-start(bf16[64,1408]{1,0:T(8,128)(2,1)S(1)} %get-tuple-element.46), channel_id=1, source_target_pairs={{0,2},{1,3},{2,0},{3,1},{4,6},{5,7},{6,4},{7,5},{8,10},{9,11},{10,... | collective-permute-start | bytes 540680 | tf_op jit(solution)/shard_map/ppermute | solution.py:343
  15.0 2.2 %shard_map.56 = (bf16[64,48,256]{2,1,0:T(8,128)(2,1)}, bf16[64,16,256]{2,1,0:T(8,128)(2,1)S(1)}) custom-call(s32[16]{0:T(128)S(1)} %fusion.3.slot_ref, bf16[8,64,1024]{2,1,0:T(8,128)(2,1)S(1)} %copy-done), custom_call_target="tpu_custom_call" | custom-call | bytes 3145728 | tf_op jit(solution)/shard_map/pallas_call | solution.py:100
  18.0 6.8 %collective-permute-done.2.p3 = bf16[64,1408]{1,0:T(8,128)(2,1)S(1)} collective-permute-done((bf16[64,1408]{1,0:T(8,128)(2,1)S(1)}, bf16[64,1408]{1,0:T(8,128)(2,1)S(1)}, u32[]{:S(2)}, u32[]{:S(2)}) %collective-permute-start.2) | collective-permute-done | bytes 180256 | tf_op jit(solution)/shard_map/ppermute | solution.py:343
  24.8 14.1 %all-to-all-start = ((bf16[64,48,256]{2,1,0:T(8,128)(2,1)}), bf16[64,48,256]{2,1,0:T(8,128)(2,1)S(1)}, u32[]{:S(2)}, u32[]{:S(2)}) async-start(bf16[64,48,256]{2,1,0:T(8,128)(2,1)} %get-tuple-element.57), calls=%async_computation | async-start | bytes 3145728 | tf_op jit(solution)/shard_map/all_to_all | solution.py:392
  39.1 2.8 %collective-permute-start.5 = (bf16[256,384]{1,0:T(8,128)(2,1)S(1)}, bf16[256,384]{1,0:T(8,128)(2,1)S(1)}, u32[]{:S(2)}, u32[]{:S(2)}) collective-permute-start(bf16[256,384]{1,0:T(8,128)(2,1)S(1)} %get-tuple-element.51), channel_id=1, source_target_pairs={{0,8},{4,12},{8,0},{12,4},{1,9},{5,13},{9,1},{13,5},{2,10},{6,14},... | collective-permute-start | bytes 589832 | tf_op jit(solution)/shard_map/ppermute | solution.py:348
  44.1 2.6 %collective-permute-done.5.far = bf16[256,384]{1,0:T(8,128)(2,1)S(1)} collective-permute-done((bf16[256,384]{1,0:T(8,128)(2,1)S(1)}, bf16[256,384]{1,0:T(8,128)(2,1)S(1)}, u32[]{:S(2)}, u32[]{:S(2)}) %collective-permute-start.5) | collective-permute-done | bytes 196640 | tf_op jit(solution)/shard_map/ppermute | solution.py:348
  46.7 4.3 %collective-permute-done.4.right = bf16[256,384]{1,0:T(8,128)(2,1)S(1)} collective-permute-done((bf16[256,384]{1,0:T(8,128)(2,1)S(1)}, bf16[256,384]{1,0:T(8,128)(2,1)S(1)}, u32[]{:S(2)}, u32[]{:S(2)}) %collective-permute-start.4) | collective-permute-done | bytes 196640 | tf_op jit(solution)/shard_map/ppermute | solution.py:348
  51.0 2.7 %shard_map.58 = (bf16[2048,128]{1,0:T(8,128)(2,1)S(1)}, f32[2048,128]{1,0:T(8,128)S(1)}, f32[2048,256]{1,0:T(8,128)S(1)}, f32[128,128]{1,0:T(8,128)S(1)}, f32[8,128]{1,0:T(8,128)S(1)}) custom-call(s32[2]{0:T(128)S(1)} %pad_add_fusion.place_ref, bf16[64,1408]{1,0:T(8,128)(2,1)S(1)} %get-tuple-element.42.p0, bf16[64,1408]{1,0:T(8,128)(2,1)S(1)} %collective-permute-done.p1, ...), custom_call_target="tpu_custom_call" | custom-call | flops 1073741824 | bytes 4194304 | tf_op jit(solution)/shard_map/pallas_call | solution.py:237
  53.7 1.3 copy-done.4
  56.1 23.7 %all-to-all-done.landed_ref = bf16[64,48,256]{2,1,0:T(8,128)(2,1)S(1)} async-done(((bf16[64,48,256]{2,1,0:T(8,128)(2,1)}), bf16[64,48,256]{2,1,0:T(8,128)(2,1)S(1)}, u32[]{:S(2)}, u32[]{:S(2)}) %all-to-all-start) | async-done | bytes 1572896 | tf_op jit(solution)/shard_map/all_to_all | solution.py:392
  80.7 2.6 %collective-permute-start.7 = (bf16[1536,256]{1,0:T(8,128)(2,1)S(1)}, bf16[1536,256]{1,0:T(8,128)(2,1)S(1)}, u32[]{:S(2)}, u32[]{:S(2)}) collective-permute-start(bf16[1536,256]{1,0:T(8,128)(2,1)S(1)} %shard_map.59.refs_0_), channel_id=1, source_target_pairs={{0,12},{4,0},{8,4},{12,8},{1,13},{5,1},{9,5},{13,9},{2,14},{6,2},{... | collective-permute-start | bytes 2359304 | tf_op jit(solution)/shard_map/ppermute | solution.py:348
  83.3 5.3 %all-to-all-start.1 = ((bf16[64,16,256]{2,1,0:T(8,128)(2,1)}), bf16[64,16,256]{2,1,0:T(8,128)(2,1)S(1)}, u32[]{:S(2)}, u32[]{:S(2)}) async-start(bf16[64,16,256]{2,1,0:T(8,128)(2,1)} %copy-done.2), calls=%async_computation.1 | async-start | bytes 1048576 | tf_op jit(solution)/shard_map/all_to_all | solution.py:392
  88.6 1.6 copy-done.5
  91.4 5.2 %shard_map.60 = (f32[2048,128]{1,0:T(8,128)S(1)}, f32[2048,256]{1,0:T(8,128)S(1)}, f32[8,128]{1,0:T(8,128)S(1)}) custom-call(f32[128,128]{1,0:T(8,128)S(1)} %get-tuple-element.52.flag_ref, bf16[2048,128]{1,0:T(8,128)(2,1)S(1)} %get-tuple-element.53.q_ref, f32[2048,128]{1,0:T(8,128)S(1)} %copy-done.7, f32[2048,256]{1,0:T(8,128)S(1)} %copy-done.5, ...), custom_call_target="tpu_custom_call" | custom-call | flops 3221225472 | bytes 8388608 | tf_op jit(solution)/shard_map/pallas_call | solution.py:308
  96.6 3.2 %collective-permute-done.7.refs_1_.right_ref = bf16[1536,256]{1,0:T(8,128)(2,1)S(1)} collective-permute-done((bf16[1536,256]{1,0:T(8,128)(2,1)S(1)}, bf16[1536,256]{1,0:T(8,128)(2,1)S(1)}, u32[]{:S(2)}, u32[]{:S(2)}) %collective-permute-start.7) | collective-permute-done | bytes 786464 | tf_op jit(solution)/shard_map/ppermute | solution.py:348
  99.9 3.7 %collective-permute-done.6.refs_0_.left_ref = bf16[1536,256]{1,0:T(8,128)(2,1)S(1)} collective-permute-done((bf16[1536,256]{1,0:T(8,128)(2,1)S(1)}, bf16[1536,256]{1,0:T(8,128)(2,1)S(1)}, u32[]{:S(2)}, u32[]{:S(2)}) %collective-permute-start.6) | collective-permute-done | bytes 786464 | tf_op jit(solution)/shard_map/ppermute | solution.py:348
  104.5 2.7 %collective-permute-start.9 = (bf16[768,256]{1,0:T(8,128)(2,1)}, bf16[768,256]{1,0:T(8,128)(2,1)}, u32[]{:S(2)}, u32[]{:S(2)}) collective-permute-start(bf16[768,256]{1,0:T(8,128)(2,1)} %get-tuple-element.65), channel_id=1, source_target_pairs={{0,12},{4,0},{8,4},{12,8},{1,13},{5,1},{9,5},{13,9},{2,14},{6,2},{... | collective-permute-start | bytes 1179656 | tf_op jit(solution)/shard_map/ppermute | solution.py:348
  107.2 9.4 %shard_map.61 = (f32[2048,128]{1,0:T(8,128)S(1)}, f32[2048,256]{1,0:T(8,128)S(1)}, f32[8,128]{1,0:T(8,128)S(1)}) custom-call(f32[128,128]{1,0:T(8,128)S(1)} %get-tuple-element.52.flag_ref, bf16[2048,128]{1,0:T(8,128)(2,1)S(1)} %get-tuple-element.53.q_ref, f32[2048,128]{1,0:T(8,128)S(1)} %get-tuple-element.59.max_in, ...), custom_call_target="tpu_custom_call" | custom-call | flops 6442450944 | bytes 8388608 | tf_op jit(solution)/shard_map/pallas_call | solution.py:308
  116.6 1.3 copy-done.8
  120.0 1.5 collective-permute-start.10
  121.4 1.6 copy-done.9
  123.0 1.2 copy-done.11
  124.2 6.2 %shard_map.63 = (f32[2048,128]{1,0:T(8,128)S(1)}, f32[2048,256]{1,0:T(8,128)S(1)}, f32[8,128]{1,0:T(8,128)S(1)}) custom-call(f32[128,128]{1,0:T(8,128)S(1)} %get-tuple-element.52.flag_ref, bf16[2048,128]{1,0:T(8,128)(2,1)S(1)} %get-tuple-element.53.q_ref, f32[2048,128]{1,0:T(8,128)S(1)} %copy-done.11, f32[2048,256]{1,0:T(8,128)S(1)} %copy-done.9, ...), custom_call_target="tpu_custom_call" | custom-call | flops 3221225472 | bytes 8388608 | tf_op jit(solution)/shard_map/pallas_call | solution.py:308
  130.6 2.7 %collective-permute-start.13 = (bf16[256,256]{1,0:T(8,128)(2,1)S(1)}, bf16[256,256]{1,0:T(8,128)(2,1)S(1)}, u32[]{:S(2)}, u32[]{:S(2)}) collective-permute-start(bf16[256,256]{1,0:T(8,128)(2,1)S(1)} %get-tuple-element.74), channel_id=1, source_target_pairs={{0,12},{4,0},{8,4},{12,8},{1,13},{5,1},{9,5},{13,9},{2,14},{6,2},{... | collective-permute-start | bytes 393224 | tf_op jit(solution)/shard_map/ppermute | solution.py:348
  133.2 5.3 %shard_map.65 = (f32[2048,128]{1,0:T(8,128)S(1)}, f32[2048,256]{1,0:T(8,128)S(1)}, f32[8,128]{1,0:T(8,128)}) custom-call(f32[128,128]{1,0:T(8,128)S(1)} %get-tuple-element.52.flag_ref, bf16[2048,128]{1,0:T(8,128)(2,1)S(1)} %get-tuple-element.53.q_ref, f32[2048,128]{1,0:T(8,128)S(1)} %get-tuple-element.66.max_in, f32[2048,256]{1,0:T(8,128)S(1)} %get-tuple-element.67.sum_in, ...), custom_call_target="tpu_custom_call" | custom-call | flops 3221225472 | bytes 8388608 | tf_op jit(solution)/shard_map/pallas_call | solution.py:308
  138.6 2.8 %shard_map.67 = (bf16[64,1024]{1,0:T(8,128)(2,1)S(1)}, bf16[64,1024]{1,0:T(8,128)(2,1)S(1)}, bf16[64,1024]{1,0:T(8,128)(2,1)S(1)}, bf16[64,1024]{1,0:T(8,128)(2,1)S(1)}) custom-call(f32[128,128]{1,0:T(8,128)S(1)} %get-tuple-element.52.flag_ref, bf16[2048,128]{1,0:T(8,128)(2,1)S(1)} %get-tuple-element.53.q_ref, f32[2048,128]{1,0:T(8,128)S(1)} %get-tuple-element.70.max_in, ...), custom_call_target="tpu_custom_call" | custom-call | flops 1073741824 | bytes 8388608 | tf_op jit(solution)/shard_map/pallas_call | solution.py:308
  141.3 1.8 %collective-permute-start.14 = (bf16[64,1024]{1,0:T(8,128)(2,1)S(1)}, bf16[64,1024]{1,0:T(8,128)(2,1)S(1)}, u32[]{:S(2)}, u32[]{:S(2)}) collective-permute-start(bf16[64,1024]{1,0:T(8,128)(2,1)S(1)} %get-tuple-element.76), channel_id=1, source_target_pairs={{0,1},{1,0},{2,3},{3,2},{4,5},{5,4},{6,7},{7,6},{8,9},{9,8},{10,11... | collective-permute-start | bytes 393224 | tf_op jit(solution)/shard_map/ppermute | solution.py:343
  143.1 2.2 %collective-permute-start.15 = (bf16[64,1024]{1,0:T(8,128)(2,1)S(1)}, bf16[64,1024]{1,0:T(8,128)(2,1)S(1)}, u32[]{:S(2)}, u32[]{:S(2)}) collective-permute-start(bf16[64,1024]{1,0:T(8,128)(2,1)S(1)} %get-tuple-element.77), channel_id=1, source_target_pairs={{0,2},{1,3},{2,0},{3,1},{4,6},{5,7},{6,4},{7,5},{8,10},{9,11},{10,... | collective-permute-start | bytes 393224 | tf_op jit(solution)/shard_map/ppermute | solution.py:343
  145.3 3.4 %collective-permute-start.16 = (bf16[64,1024]{1,0:T(8,128)(2,1)S(1)}, bf16[64,1024]{1,0:T(8,128)(2,1)S(1)}, u32[]{:S(2)}, u32[]{:S(2)}) collective-permute-start(bf16[64,1024]{1,0:T(8,128)(2,1)S(1)} %get-tuple-element.78), channel_id=1, source_target_pairs={{0,3},{1,2},{2,1},{3,0},{4,7},{5,6},{6,5},{7,4},{8,11},{9,10},{10,... | collective-permute-start | bytes 393224 | tf_op jit(solution)/shard_map/ppermute | solution.py:343
  148.7 5.8 %collective-permute-done.15.refs_2_ = bf16[64,1024]{1,0:T(8,128)(2,1)S(1)} collective-permute-done((bf16[64,1024]{1,0:T(8,128)(2,1)S(1)}, bf16[64,1024]{1,0:T(8,128)(2,1)S(1)}, u32[]{:S(2)}, u32[]{:S(2)}) %collective-permute-start.15) | collective-permute-done | bytes 131104 | tf_op jit(solution)/shard_map/ppermute | solution.py:343
  154.5 5.1 %collective-permute-done.16.refs_3_ = bf16[64,1024]{1,0:T(8,128)(2,1)S(1)} collective-permute-done((bf16[64,1024]{1,0:T(8,128)(2,1)S(1)}, bf16[64,1024]{1,0:T(8,128)(2,1)S(1)}, u32[]{:S(2)}, u32[]{:S(2)}) %collective-permute-start.16) | collective-permute-done | bytes 131104 | tf_op jit(solution)/shard_map/ppermute | solution.py:343
  (57 shorter events, 16.7 us)
Async XLA Ops:
  1.6 1.0 copy-start.1
  2.6 0.9 copy-start.3
  4.1 13.9 %collective-permute-start = (bf16[64,1408]{1,0:T(8,128)(2,1)S(1)}, bf16[64,1408]{1,0:T(8,128)(2,1)S(1)}, u32[]{:S(2)}, u32[]{:S(2)}) collective-permute-start(bf16[64,1408]{1,0:T(8,128)(2,1)S(1)} %get-tuple-element.45), channel_id=1, source_target_pairs={{0,1},{1,0},{2,3},{3,2},{4,5},{5,4},{6,7},{7,6},{8,9},{9,8},{10,11... | collective-permute-start | bytes 540680 | tf_op jit(solution)/shard_map/ppermute | solution.py:343
  7.5 10.5 %collective-permute-start.1 = (bf16[64,1408]{1,0:T(8,128)(2,1)S(1)}, bf16[64,1408]{1,0:T(8,128)(2,1)S(1)}, u32[]{:S(2)}, u32[]{:S(2)}) collective-permute-start(bf16[64,1408]{1,0:T(8,128)(2,1)S(1)} %get-tuple-element.46), channel_id=1, source_target_pairs={{0,2},{1,3},{2,0},{3,1},{4,6},{5,7},{6,4},{7,5},{8,10},{9,11},{10,... | collective-permute-start | bytes 540680 | tf_op jit(solution)/shard_map/ppermute | solution.py:343
  12.7 12.2 %collective-permute-start.2 = (bf16[64,1408]{1,0:T(8,128)(2,1)S(1)}, bf16[64,1408]{1,0:T(8,128)(2,1)S(1)}, u32[]{:S(2)}, u32[]{:S(2)}) collective-permute-start(bf16[64,1408]{1,0:T(8,128)(2,1)S(1)} %get-tuple-element.47), channel_id=1, source_target_pairs={{0,3},{1,2},{2,1},{3,0},{4,7},{5,6},{6,5},{7,4},{8,11},{9,10},{10,... | collective-permute-start | bytes 540680 | tf_op jit(solution)/shard_map/ppermute | solution.py:343
  13.8 1.2 copy-start
  17.2 0.8 copy-start.2
  24.8 54.9 %all-to-all-start = ((bf16[64,48,256]{2,1,0:T(8,128)(2,1)}), bf16[64,48,256]{2,1,0:T(8,128)(2,1)S(1)}, u32[]{:S(2)}, u32[]{:S(2)}) async-start(bf16[64,48,256]{2,1,0:T(8,128)(2,1)} %get-tuple-element.57), calls=%async_computation | async-start | bytes 3145728 | tf_op jit(solution)/shard_map/all_to_all | solution.py:392
  39.1 7.6 %collective-permute-start.5 = (bf16[256,384]{1,0:T(8,128)(2,1)S(1)}, bf16[256,384]{1,0:T(8,128)(2,1)S(1)}, u32[]{:S(2)}, u32[]{:S(2)}) collective-permute-start(bf16[256,384]{1,0:T(8,128)(2,1)S(1)} %get-tuple-element.51), channel_id=1, source_target_pairs={{0,8},{4,12},{8,0},{12,4},{1,9},{5,13},{9,1},{13,5},{2,10},{6,14},... | collective-permute-start | bytes 589832 | tf_op jit(solution)/shard_map/ppermute | solution.py:348
  41.9 9.1 %collective-permute-start.4 = (bf16[256,384]{1,0:T(8,128)(2,1)S(1)}, bf16[256,384]{1,0:T(8,128)(2,1)S(1)}, u32[]{:S(2)}, u32[]{:S(2)}) collective-permute-start(bf16[256,384]{1,0:T(8,128)(2,1)S(1)} %get-tuple-element.51), channel_id=1, source_target_pairs={{0,12},{4,0},{8,4},{12,8},{1,13},{5,1},{9,5},{13,9},{2,14},{6,2},{... | collective-permute-start | bytes 589832 | tf_op jit(solution)/shard_map/ppermute | solution.py:348
  42.8 8.3 %collective-permute-start.3 = (bf16[256,384]{1,0:T(8,128)(2,1)S(1)}, bf16[256,384]{1,0:T(8,128)(2,1)S(1)}, u32[]{:S(2)}, u32[]{:S(2)}) collective-permute-start(bf16[256,384]{1,0:T(8,128)(2,1)S(1)} %get-tuple-element.51), channel_id=1, source_target_pairs={{0,4},{4,8},{8,12},{12,0},{1,5},{5,9},{9,13},{13,1},{2,6},{6,10},{... | collective-permute-start | bytes 589832 | tf_op jit(solution)/shard_map/ppermute | solution.py:348
  53.7 1.3 copy-start.4
  55.1 1.0 copy-start.6
  80.7 19.1 %collective-permute-start.7 = (bf16[1536,256]{1,0:T(8,128)(2,1)S(1)}, bf16[1536,256]{1,0:T(8,128)(2,1)S(1)}, u32[]{:S(2)}, u32[]{:S(2)}) collective-permute-start(bf16[1536,256]{1,0:T(8,128)(2,1)S(1)} %shard_map.59.refs_0_), channel_id=1, source_target_pairs={{0,12},{4,0},{8,4},{12,8},{1,13},{5,1},{9,5},{13,9},{2,14},{6,2},{... | collective-permute-start | bytes 2359304 | tf_op jit(solution)/shard_map/ppermute | solution.py:348
  83.3 20.3 %collective-permute-start.6 = (bf16[1536,256]{1,0:T(8,128)(2,1)S(1)}, bf16[1536,256]{1,0:T(8,128)(2,1)S(1)}, u32[]{:S(2)}, u32[]{:S(2)}) collective-permute-start(bf16[1536,256]{1,0:T(8,128)(2,1)S(1)} %shard_map.59.refs_0_), channel_id=1, source_target_pairs={{0,4},{4,8},{8,12},{12,0},{1,5},{5,9},{9,13},{13,1},{2,6},{6,10},{... | collective-permute-start | bytes 2359304 | tf_op jit(solution)/shard_map/ppermute | solution.py:348
  83.3 35.6 %all-to-all-start.1 = ((bf16[64,16,256]{2,1,0:T(8,128)(2,1)}), bf16[64,16,256]{2,1,0:T(8,128)(2,1)S(1)}, u32[]{:S(2)}, u32[]{:S(2)}) async-start(bf16[64,16,256]{2,1,0:T(8,128)(2,1)} %copy-done.2), calls=%async_computation.1 | async-start | bytes 1048576 | tf_op jit(solution)/shard_map/all_to_all | solution.py:392
  88.6 1.6 copy-start.5
  90.2 1.2 copy-start.7
  104.5 16.9 %collective-permute-start.8 = (bf16[768,256]{1,0:T(8,128)(2,1)}, bf16[768,256]{1,0:T(8,128)(2,1)S(1)}, u32[]{:S(2)}, u32[]{:S(2)}) collective-permute-start(bf16[768,256]{1,0:T(8,128)(2,1)} %get-tuple-element.64), channel_id=1, source_target_pairs={{0,4},{4,8},{8,12},{12,0},{1,5},{5,9},{9,13},{13,1},{2,6},{6,10},{... | collective-permute-start | bytes 1179656 | tf_op jit(solution)/shard_map/ppermute | solution.py:348
  104.5 16.9 %collective-permute-start.9 = (bf16[768,256]{1,0:T(8,128)(2,1)}, bf16[768,256]{1,0:T(8,128)(2,1)}, u32[]{:S(2)}, u32[]{:S(2)}) collective-permute-start(bf16[768,256]{1,0:T(8,128)(2,1)} %get-tuple-element.65), channel_id=1, source_target_pairs={{0,12},{4,0},{8,4},{12,8},{1,13},{5,1},{9,5},{13,9},{2,14},{6,2},{... | collective-permute-start | bytes 1179656 | tf_op jit(solution)/shard_map/ppermute | solution.py:348
  116.6 1.3 copy-start.8
  117.9 1.0 copy-start.10
  119.9 10.6 %collective-permute-start.11 = (bf16[512,256]{1,0:T(8,128)(2,1)S(1)}, bf16[512,256]{1,0:T(8,128)(2,1)S(1)}, u32[]{:S(2)}, u32[]{:S(2)}) collective-permute-start(bf16[512,256]{1,0:T(8,128)(2,1)S(1)} %shard_map.64.refs_0_), channel_id=1, source_target_pairs={{0,12},{4,0},{8,4},{12,8},{1,13},{5,1},{9,5},{13,9},{2,14},{6,2},{... | collective-permute-start | bytes 786440 | tf_op jit(solution)/shard_map/ppermute | solution.py:348
  120.0 10.5 %collective-permute-start.10 = (bf16[512,256]{1,0:T(8,128)(2,1)S(1)}, bf16[512,256]{1,0:T(8,128)(2,1)S(1)}, u32[]{:S(2)}, u32[]{:S(2)}) collective-permute-start(bf16[512,256]{1,0:T(8,128)(2,1)S(1)} %shard_map.64.refs_0_), channel_id=1, source_target_pairs={{0,4},{4,8},{8,12},{12,0},{1,5},{5,9},{9,13},{13,1},{2,6},{6,10},{... | collective-permute-start | bytes 786440 | tf_op jit(solution)/shard_map/ppermute | solution.py:348
  121.4 1.6 copy-start.9
  123.0 1.2 copy-start.11
  130.5 8.1 %collective-permute-start.12 = (bf16[256,256]{1,0:T(8,128)(2,1)S(1)}, bf16[256,256]{1,0:T(8,128)(2,1)S(1)}, u32[]{:S(2)}, u32[]{:S(2)}) collective-permute-start(bf16[256,256]{1,0:T(8,128)(2,1)S(1)} %get-tuple-element.73), channel_id=1, source_target_pairs={{0,4},{4,8},{8,12},{12,0},{1,5},{5,9},{9,13},{13,1},{2,6},{6,10},{... | collective-permute-start | bytes 393224 | tf_op jit(solution)/shard_map/ppermute | solution.py:348
  130.6 8.0 %collective-permute-start.13 = (bf16[256,256]{1,0:T(8,128)(2,1)S(1)}, bf16[256,256]{1,0:T(8,128)(2,1)S(1)}, u32[]{:S(2)}, u32[]{:S(2)}) collective-permute-start(bf16[256,256]{1,0:T(8,128)(2,1)S(1)} %get-tuple-element.74), channel_id=1, source_target_pairs={{0,12},{4,0},{8,4},{12,8},{1,13},{5,1},{9,5},{13,9},{2,14},{6,2},{... | collective-permute-start | bytes 393224 | tf_op jit(solution)/shard_map/ppermute | solution.py:348
  141.3 7.4 %collective-permute-start.14 = (bf16[64,1024]{1,0:T(8,128)(2,1)S(1)}, bf16[64,1024]{1,0:T(8,128)(2,1)S(1)}, u32[]{:S(2)}, u32[]{:S(2)}) collective-permute-start(bf16[64,1024]{1,0:T(8,128)(2,1)S(1)} %get-tuple-element.76), channel_id=1, source_target_pairs={{0,1},{1,0},{2,3},{3,2},{4,5},{5,4},{6,7},{7,6},{8,9},{9,8},{10,11... | collective-permute-start | bytes 393224 | tf_op jit(solution)/shard_map/ppermute | solution.py:343
  143.1 11.4 %collective-permute-start.15 = (bf16[64,1024]{1,0:T(8,128)(2,1)S(1)}, bf16[64,1024]{1,0:T(8,128)(2,1)S(1)}, u32[]{:S(2)}, u32[]{:S(2)}) collective-permute-start(bf16[64,1024]{1,0:T(8,128)(2,1)S(1)} %get-tuple-element.77), channel_id=1, source_target_pairs={{0,2},{1,3},{2,0},{3,1},{4,6},{5,7},{6,4},{7,5},{8,10},{9,11},{10,... | collective-permute-start | bytes 393224 | tf_op jit(solution)/shard_map/ppermute | solution.py:343
  145.3 14.3 %collective-permute-start.16 = (bf16[64,1024]{1,0:T(8,128)(2,1)S(1)}, bf16[64,1024]{1,0:T(8,128)(2,1)S(1)}, u32[]{:S(2)}, u32[]{:S(2)}) collective-permute-start(bf16[64,1024]{1,0:T(8,128)(2,1)S(1)} %get-tuple-element.78), channel_id=1, source_target_pairs={{0,3},{1,2},{2,1},{3,0},{4,7},{5,6},{6,5},{7,4},{8,11},{9,10},{10,... | collective-permute-start | bytes 393224 | tf_op jit(solution)/shard_map/ppermute | solution.py:343

commit v3 on v2

--- a/solution.py
+++ b/solution.py
@@ -25,7 +25,7 @@
 UNROLL = 4
 EXP2_SCALE = math.log2(math.e) / math.sqrt(HD)
 LOWEST = -1e30
-CHUNKS = (48, 16)
+CHUNKS = (64,)
 KEY_TILE = 1024
 
 AXES = ("zlo", "y", "x", "zhi", "core")
@@ -125,29 +125,31 @@
     )(*pieces)
 
 
-def pack_kernel(slot_ref, flag_ref, landed_ref, token_ref, out_ref):
+def pack_kernel(slot_ref, flag_ref, landed_ref, token_ref, *outs):
     tokens = landed_ref.shape[1]
-
-    def one(entry, carry):
-        rows = columns(entry, tokens)
-        out_ref[rows, :] = landed_ref[slot_ref[entry]]
-
-        @pl.when(flag_ref[entry] == 0)
-        def _():
-            out_ref[rows, HD:] = jnp.zeros((tokens, HD), BF16)
-
-        return carry
-
-    lax.fori_loop(0, 4 * LOCAL, one, 0)
+    for part, out in enumerate(outs):
+
+        def one(place, carry, part=part, out=out):
+            entry = part * 2 * LOCAL + place
+            rows = columns(place, tokens)
+            out[rows, :] = landed_ref[slot_ref[entry]]
+
+            @pl.when(flag_ref[entry] == 0)
+            def _():
+                out[rows, HD:] = jnp.zeros((tokens, HD), BF16)
+
+            return carry
+
+        lax.fori_loop(0, 2 * LOCAL, one, 0)
 
 
 def pack_blocks(slots, flags, landed, token):
     tokens = landed.shape[1]
     return pl.pallas_call(
         pack_kernel,
-        out_shape=bf16_shape(4 * LOCAL * tokens, 2 * HD),
+        out_shape=[bf16_shape(2 * LOCAL * tokens, 2 * HD)] * 2,
         in_specs=[SMEM, SMEM, VMEM, VMEM],
-        out_specs=VMEM,
+        out_specs=[VMEM] * 2,
         compiler_params=params(16),
         cost_estimate=cost(0, 3 << 20),
     )(slots, flags, landed, token)
@@ -243,23 +245,6 @@
         compiler_params=params(),
         cost_estimate=cost(4 * ALL_ROWS * 1024 * HD, 4 << 20),
     )(place, *pieces, left, right, far)
-
-
-def halves_kernel(left_ref, right_ref, token_ref, left_out, right_out):
-    middle = left_out.shape[0]
-    left_out[...] = left_ref[:middle, :]
-    right_out[...] = right_ref[middle:, :]
-
-
-def halves(left, right, token):
-    return pl.pallas_call(
-        halves_kernel,
-        out_shape=[bf16_shape(left.shape[0] // 2, 2 * HD)] * 2,
-        in_specs=[VMEM] * 3,
-        out_specs=[VMEM] * 2,
-        compiler_params=params(16),
-        cost_estimate=cost(0, 1 << 20),
-    )(left, right, token)
 
 
 def passage_kernel(layout, last, flag_ref, q_ref, max_in, sum_in, *refs):
@@ -384,30 +369,20 @@
         along("x", question, 2),
     )
 
-    quarter, half = 4 * LOCAL, 2 * LOCAL
-    own_flags, left_flags, right_flags = [(i * quarter, quarter) for i in range(3)]
-    far_flags = ((3 * quarter, half), (3 * quarter + half, half))
-
-    def fetch(chunk, token):
-        landed = lax.all_to_all(outgoing[chunk], SEND_AXES, 0, 0, tiled=True)
-        own = pack_blocks(landed_slots, landed_flags, landed, token)
-        return own, along("x", own, 1), along("x", own, 3)
-
-    def relay(left, right, token):
-        first, second = halves(left, right, token)
-        return along("x", first, 1), along("x", second, 3)
-
+    landed = lax.all_to_all(outgoing[0], SEND_AXES, 0, 0, tiled=True)
+    own_a, own_b = pack_blocks(landed_slots, landed_flags, landed, token)
+    left_a, right_b = along("x", own_a, 1), along("x", own_b, 3)
+    left_b, right_a = along("x", own_b, 1), along("x", own_a, 3)
+
+    half = 2 * LOCAL
+    layouts = [((i * half, half), (j * half, half)) for i, j in ((0, 1), (2, 5), (3, 4), (6, 7))]
     attend = functools.partial(passage_part, flags, query)
-    own, left, right = fetch(0, token)
-    *state, token = attend(state, (own,), (own_flags,), False)
-    far = relay(left, right, token)
-    *state, token = attend(state, (left, right), (left_flags, right_flags), False)
-    own, left, right = fetch(1, token)
-    *state, token = attend(state, far, far_flags, False)
-    far = relay(left, right, token)
-    layout = (own_flags, left_flags, right_flags)
-    *state, token = attend(state, (own, left, right), layout, False)
-    state = attend(state, far, far_flags, True)
+    *state, _ = attend(state, (own_a, own_b), layouts[0], False)
+    left_a, right_b, *state = lax.optimization_barrier((left_a, right_b, *state))
+    far_a, far_b = along("x", left_a, 1), along("x", right_b, 3)
+    *state, _ = attend(state, (left_a, right_b), layouts[1], False)
+    *state, _ = attend(state, (left_b, right_a), layouts[2], False)
+    state = attend(state, (far_a, far_b), layouts[3], True)
 
     return join_outputs(ints(head), swap_heads(state))
 

time: 161 us -> 153 us (0.950)
  waiting for transfers between devices: 55.3 us -> 66.3 us
  starting transfers between devices: 49.6 us -> 40.3 us
  local copies, waits for them, and re-layouts: 16.2 us -> 10.5 us
  Pallas kernels: 38.1 us -> 34.6 us
    all_to_all x2 -> x1, waiting for transfers between devices: 23.7 us -> 32.3 us  [body(): landed = lax.all_to_all(outgoing[0], SEND_AXES, 0, 0, tiled=True)]
    unnamed x25 -> x19, local copies, waits for them, and re-layouts: 14.9 us -> 9.29 us
    all_to_all x2 -> x1, starting transfers between devices: 19.4 us -> 14.1 us  [body(): landed = lax.all_to_all(outgoing[0], SEND_AXES, 0, 0, tiled=True)]
    ppermute x11 -> x9, starting transfers between devices: 13.8 us -> 11.1 us  [along(): return lax.ppermute(value, axis, [(i, (i + hops) % 4) for i in range(4)])]
    pallas_call x5 -> x4, Pallas kernels: 28.8 us -> 26.4 us  [passage_part(): pl.pallas_call(functools.partial(passage_kernel, layout, last), out_shape...]
    pallas_call x4 -> x1, Pallas kernels: 2.91 us -> 1 us  [pack_blocks(): pl.pallas_call(pack_kernel, out_shape=[bf16_shape(2 * LOCAL * tokens, 2 *...]
    ppermute x11 -> x9, waiting for transfers between devices: 13.9 us -> 15.8 us  [along(): return lax.ppermute(value, axis, [(i, (i + hops) % 4) for i in range(4)])]
  transfers between devices with their start and end apart: 19 -> 16, of which waited for: 8 -> 11; matrix products, arithmetic and copies ran while one was open for 1% -> 1% of each run, Pallas kernels for 20% -> 17%
where the time goes in v3:
time: 153 us
  waiting for transfers between devices  66.3 us (43%)
  starting transfers between devices  40.3 us (26%)
  Pallas kernels  34.6 us (23%)
  local copies, waits for them, and re-layouts  10.5 us (7%)
    all_to_all x1, waiting for transfers between devices, body(): landed = lax.all_to_all(outgoing[0], SEND_AXES, 0, 0, tiled=True)  32.3 us
    pallas_call x4, Pallas kernels, passage_part(): pl.pallas_call(functools.partial(passage_kernel, layout, last), out_shape...  26.4 us
    ppermute x6, waiting for transfers between devices, swap_heads(): moved.append(lax.ppermute(pieces[offset], HEAD_AXES, pairs))  18.3 us
    ppermute x9, waiting for transfers between devices, along(): return lax.ppermute(value, axis, [(i, (i + hops) % 4) for i in range(4)])  15.8 us
    ppermute x6, starting transfers between devices, swap_heads(): moved.append(lax.ppermute(pieces[offset], HEAD_AXES, pairs))  15.1 us
    all_to_all x1, starting transfers between devices, body(): landed = lax.all_to_all(outgoing[0], SEND_AXES, 0, 0, tiled=True)  14.1 us
    ppermute x9, starting transfers between devices, along(): return lax.ppermute(value, axis, [(i, (i + hops) % 4) for i in range(4)])  11.1 us
    unnamed x19, local copies, waits for them, and re-layouts  9.29 us
  transfers between devices with their start and end apart: 16, of which 11 were waited for; matrix products, arithmetic and copies ran while one was open for 1% of the time, Pallas kernels for 17%

profile of v3, /device:TPU:1, one launch (start us, length us, event | category | flops | bytes accessed | tf_op | source)
XLA Modules:
  0.0 153.0 jit_solution(657999605219924544)
XLA Ops:
  1.6 1.0 copy-done.1
  4.1 3.3 %collective-permute-start = (bf16[64,1408]{1,0:T(8,128)(2,1)S(1)}, bf16[64,1408]{1,0:T(8,128)(2,1)S(1)}, u32[]{:S(2)}, u32[]{:S(2)}) collective-permute-start(bf16[64,1408]{1,0:T(8,128)(2,1)S(1)} %get-tuple-element.37), channel_id=1, source_target_pairs={{0,1},{1,0},{2,3},{3,2},{4,5},{5,4},{6,7},{7,6},{8,9},{9,8},{10,11... | collective-permute-start | bytes 540680 | tf_op jit(solution)/shard_map/ppermute | solution.py:328
  7.5 5.2 %collective-permute-start.1 = (bf16[64,1408]{1,0:T(8,128)(2,1)S(1)}, bf16[64,1408]{1,0:T(8,128)(2,1)S(1)}, u32[]{:S(2)}, u32[]{:S(2)}) collective-permute-start(bf16[64,1408]{1,0:T(8,128)(2,1)S(1)} %get-tuple-element.38), channel_id=1, source_target_pairs={{0,2},{1,3},{2,0},{3,1},{4,6},{5,7},{6,4},{7,5},{8,10},{9,11},{10,... | collective-permute-start | bytes 540680 | tf_op jit(solution)/shard_map/ppermute | solution.py:328
  13.8 1.2 copy-done
  15.0 2.3 %shard_map.56 = bf16[64,64,256]{2,1,0:T(8,128)(2,1)} custom-call(s32[16]{0:T(128)S(1)} %fusion.3.slot_ref, bf16[8,64,1024]{2,1,0:T(8,128)(2,1)S(1)} %copy-done), custom_call_target="tpu_custom_call" | custom-call | bytes 3145728 | tf_op jit(solution)/shard_map/pallas_call | solution.py:100
  17.5 7.3 %collective-permute-done.2.p3 = bf16[64,1408]{1,0:T(8,128)(2,1)S(1)} collective-permute-done((bf16[64,1408]{1,0:T(8,128)(2,1)S(1)}, bf16[64,1408]{1,0:T(8,128)(2,1)S(1)}, u32[]{:S(2)}, u32[]{:S(2)}) %collective-permute-start.2) | collective-permute-done | bytes 180256 | tf_op jit(solution)/shard_map/ppermute | solution.py:328
  24.8 14.1 %all-to-all-start = ((bf16[64,64,256]{2,1,0:T(8,128)(2,1)}), bf16[64,64,256]{2,1,0:T(8,128)(2,1)S(1)}, u32[]{:S(2)}, u32[]{:S(2)}) async-start(bf16[64,64,256]{2,1,0:T(8,128)(2,1)} %shard_map.56), calls=%async_computation | async-start | bytes 4194304 | tf_op jit(solution)/shard_map/all_to_all | solution.py:372
  39.7 2.7 %collective-permute-start.5 = (bf16[256,384]{1,0:T(8,128)(2,1)}, bf16[256,384]{1,0:T(8,128)(2,1)S(1)}, u32[]{:S(2)}, u32[]{:S(2)}) collective-permute-start(bf16[256,384]{1,0:T(8,128)(2,1)} %get-tuple-element.43), channel_id=1, source_target_pairs={{0,8},{4,12},{8,0},{12,4},{1,9},{5,13},{9,1},{13,5},{2,10},{6,14},... | collective-permute-start | bytes 589832 | tf_op jit(solution)/shard_map/ppermute | solution.py:333
  44.6 2.8 %collective-permute-done.5.far = bf16[256,384]{1,0:T(8,128)(2,1)S(1)} collective-permute-done((bf16[256,384]{1,0:T(8,128)(2,1)}, bf16[256,384]{1,0:T(8,128)(2,1)S(1)}, u32[]{:S(2)}, u32[]{:S(2)}) %collective-permute-start.5) | collective-permute-done | bytes 196640 | tf_op jit(solution)/shard_map/ppermute | solution.py:333
  47.5 4.3 %collective-permute-done.4.right = bf16[256,384]{1,0:T(8,128)(2,1)S(1)} collective-permute-done((bf16[256,384]{1,0:T(8,128)(2,1)}, bf16[256,384]{1,0:T(8,128)(2,1)S(1)}, u32[]{:S(2)}, u32[]{:S(2)}) %collective-permute-start.4) | collective-permute-done | bytes 196640 | tf_op jit(solution)/shard_map/ppermute | solution.py:333
  51.8 2.7 %shard_map.58 = (bf16[2048,128]{1,0:T(8,128)(2,1)S(1)}, f32[2048,128]{1,0:T(8,128)S(1)}, f32[2048,256]{1,0:T(8,128)S(1)}, f32[128,128]{1,0:T(8,128)S(1)}, f32[8,128]{1,0:T(8,128)S(1)}) custom-call(s32[2]{0:T(128)S(1)} %pad_add_fusion.place_ref, bf16[64,1408]{1,0:T(8,128)(2,1)S(1)} %get-tuple-element.36.p0, bf16[64,1408]{1,0:T(8,128)(2,1)S(1)} %collective-permute-done.p1, ...), custom_call_target="tpu_custom_call" | custom-call | flops 1073741824 | bytes 4194304 | tf_op jit(solution)/shard_map/pallas_call | solution.py:239
  54.5 1.3 copy-done.3
  55.9 1.0 copy-done.5
  57.7 32.3 %all-to-all-done.landed_ref = bf16[64,64,256]{2,1,0:T(8,128)(2,1)S(1)} async-done(((bf16[64,64,256]{2,1,0:T(8,128)(2,1)}), bf16[64,64,256]{2,1,0:T(8,128)(2,1)S(1)}, u32[]{:S(2)}, u32[]{:S(2)}) %all-to-all-start) | async-done | bytes 2097184 | tf_op jit(solution)/shard_map/all_to_all | solution.py:372
  91.0 1.3 collective-permute-start.6
  92.3 1.5 collective-permute-start.7
  93.7 1.3 collective-permute-start.9
  95.2 1.2 copy-done.6
  96.5 1.0 copy-done.8
  97.5 6.6 %shard_map.60 = (f32[2048,128]{1,0:T(8,128)S(1)}, f32[2048,256]{1,0:T(8,128)S(1)}, f32[8,128]{1,0:T(8,128)}) custom-call(f32[128,128]{1,0:T(8,128)S(1)} %get-tuple-element.44.flag_ref, bf16[2048,128]{1,0:T(8,128)(2,1)S(1)} %copy-done.8, f32[2048,128]{1,0:T(8,128)S(1)} %copy-done.6, f32[2048,256]{1,0:T(8,128)S(1)} %copy-done.4, ...), custom_call_target="tpu_custom_call" | custom-call | flops 4294967296 | bytes 8388608 | tf_op jit(solution)/shard_map/pallas_call | solution.py:293
  104.1 2.1 %collective-permute-done.6.refs_0_ = bf16[1024,256]{1,0:T(8,128)(2,1)S(1)} collective-permute-done((bf16[1024,256]{1,0:T(8,128)(2,1)S(1)}, bf16[1024,256]{1,0:T(8,128)(2,1)S(1)}, u32[]{:S(2)}, u32[]{:S(2)}) %collective-permute-start.6) | collective-permute-done | bytes 524320 | tf_op jit(solution)/shard_map/ppermute | solution.py:333
  106.2 1.2 collective-permute-start.10
  107.4 1.5 collective-permute-start.11
  108.9 6.7 %shard_map.61 = (f32[2048,128]{1,0:T(8,128)S(1)}, f32[2048,256]{1,0:T(8,128)S(1)}, f32[8,128]{1,0:T(8,128)}) custom-call(f32[128,128]{1,0:T(8,128)S(1)} %get-tuple-element.44.flag_ref, bf16[2048,128]{1,0:T(8,128)(2,1)S(1)} %copy-done.8, f32[2048,128]{1,0:T(8,128)S(1)} %get-tuple-element.55.max_in, f32[2048,256]{1,0:T(8,128)S(1)} %get-tuple-element.56.sum_in, ...), custom_call_target="tpu_custom_call" | custom-call | flops 4294967296 | bytes 8388608 | tf_op jit(solution)/shard_map/pallas_call | solution.py:293
  115.6 1.9 %collective-permute-done.9.refs_1_ = bf16[1024,256]{1,0:T(8,128)(2,1)S(1)} collective-permute-done((bf16[1024,256]{1,0:T(8,128)(2,1)S(1)}, bf16[1024,256]{1,0:T(8,128)(2,1)S(1)}, u32[]{:S(2)}, u32[]{:S(2)}) %collective-permute-start.9) | collective-permute-done | bytes 524320 | tf_op jit(solution)/shard_map/ppermute | solution.py:333
  117.4 6.6 %shard_map.62 = (f32[2048,128]{1,0:T(8,128)S(1)}, f32[2048,256]{1,0:T(8,128)S(1)}, f32[8,128]{1,0:T(8,128)}) custom-call(f32[128,128]{1,0:T(8,128)S(1)} %get-tuple-element.44.flag_ref, bf16[2048,128]{1,0:T(8,128)(2,1)S(1)} %copy-done.8, f32[2048,128]{1,0:T(8,128)S(1)} %get-tuple-element.59.max_in, f32[2048,256]{1,0:T(8,128)S(1)} %get-tuple-element.60.sum_in, ...), custom_call_target="tpu_custom_call" | custom-call | flops 4294967296 | bytes 8388608 | tf_op jit(solution)/shard_map/pallas_call | solution.py:293
  124.1 4.1 %collective-permute-done.10.refs_0_ = bf16[1024,256]{1,0:T(8,128)(2,1)S(1)} collective-permute-done((bf16[1024,256]{1,0:T(8,128)(2,1)S(1)}, bf16[1024,256]{1,0:T(8,128)(2,1)S(1)}, u32[]{:S(2)}, u32[]{:S(2)}) %collective-permute-start.10) | collective-permute-done | bytes 524320 | tf_op jit(solution)/shard_map/ppermute | solution.py:333
  128.7 6.6 %shard_map.63 = (bf16[64,1024]{1,0:T(8,128)(2,1)S(1)}, bf16[64,1024]{1,0:T(8,128)(2,1)S(1)}, bf16[64,1024]{1,0:T(8,128)(2,1)S(1)}, bf16[64,1024]{1,0:T(8,128)(2,1)S(1)}) custom-call(f32[128,128]{1,0:T(8,128)S(1)} %get-tuple-element.44.flag_ref, bf16[2048,128]{1,0:T(8,128)(2,1)S(1)} %copy-done.8, f32[2048,128]{1,0:T(8,128)S(1)} %get-tuple-element.61.max_in, ...), custom_call_target="tpu_custom_call" | custom-call | flops 4294967296 | bytes 8388608 | tf_op jit(solution)/shard_map/pallas_call | solution.py:293
  135.7 2.2 %collective-permute-start.13 = (bf16[64,1024]{1,0:T(8,128)(2,1)S(1)}, bf16[64,1024]{1,0:T(8,128)(2,1)S(1)}, u32[]{:S(2)}, u32[]{:S(2)}) collective-permute-start(bf16[64,1024]{1,0:T(8,128)(2,1)S(1)} %get-tuple-element.65), channel_id=1, source_target_pairs={{0,2},{1,3},{2,0},{3,1},{4,6},{5,7},{6,4},{7,5},{8,10},{9,11},{10,... | collective-permute-start | bytes 393224 | tf_op jit(solution)/shard_map/ppermute | solution.py:328
  138.0 3.4 %collective-permute-start.14 = (bf16[64,1024]{1,0:T(8,128)(2,1)S(1)}, bf16[64,1024]{1,0:T(8,128)(2,1)S(1)}, u32[]{:S(2)}, u32[]{:S(2)}) collective-permute-start(bf16[64,1024]{1,0:T(8,128)(2,1)S(1)} %get-tuple-element.66), channel_id=1, source_target_pairs={{0,3},{1,2},{2,1},{3,0},{4,7},{5,6},{6,5},{7,4},{8,11},{9,10},{10,... | collective-permute-start | bytes 393224 | tf_op jit(solution)/shard_map/ppermute | solution.py:328
  141.4 5.7 %collective-permute-done.13.refs_2_ = bf16[64,1024]{1,0:T(8,128)(2,1)S(1)} collective-permute-done((bf16[64,1024]{1,0:T(8,128)(2,1)S(1)}, bf16[64,1024]{1,0:T(8,128)(2,1)S(1)}, u32[]{:S(2)}, u32[]{:S(2)}) %collective-permute-start.13) | collective-permute-done | bytes 131104 | tf_op jit(solution)/shard_map/ppermute | solution.py:328
  147.1 5.1 %collective-permute-done.14.refs_3_ = bf16[64,1024]{1,0:T(8,128)(2,1)S(1)} collective-permute-done((bf16[64,1024]{1,0:T(8,128)(2,1)S(1)}, bf16[64,1024]{1,0:T(8,128)(2,1)S(1)}, u32[]{:S(2)}, u32[]{:S(2)}) %collective-permute-start.14) | collective-permute-done | bytes 131104 | tf_op jit(solution)/shard_map/ppermute | solution.py:328
  (41 shorter events, 11.2 us)
Async XLA Ops:
  1.6 1.0 copy-start.1
  2.6 0.9 copy-start.2
  4.1 13.2 %collective-permute-start = (bf16[64,1408]{1,0:T(8,128)(2,1)S(1)}, bf16[64,1408]{1,0:T(8,128)(2,1)S(1)}, u32[]{:S(2)}, u32[]{:S(2)}) collective-permute-start(bf16[64,1408]{1,0:T(8,128)(2,1)S(1)} %get-tuple-element.37), channel_id=1, source_target_pairs={{0,1},{1,0},{2,3},{3,2},{4,5},{5,4},{6,7},{7,6},{8,9},{9,8},{10,11... | collective-permute-start | bytes 540680 | tf_op jit(solution)/shard_map/ppermute | solution.py:328
  7.5 10.0 %collective-permute-start.1 = (bf16[64,1408]{1,0:T(8,128)(2,1)S(1)}, bf16[64,1408]{1,0:T(8,128)(2,1)S(1)}, u32[]{:S(2)}, u32[]{:S(2)}) collective-permute-start(bf16[64,1408]{1,0:T(8,128)(2,1)S(1)} %get-tuple-element.38), channel_id=1, source_target_pairs={{0,2},{1,3},{2,0},{3,1},{4,6},{5,7},{6,4},{7,5},{8,10},{9,11},{10,... | collective-permute-start | bytes 540680 | tf_op jit(solution)/shard_map/ppermute | solution.py:328
  12.7 12.2 %collective-permute-start.2 = (bf16[64,1408]{1,0:T(8,128)(2,1)S(1)}, bf16[64,1408]{1,0:T(8,128)(2,1)S(1)}, u32[]{:S(2)}, u32[]{:S(2)}) collective-permute-start(bf16[64,1408]{1,0:T(8,128)(2,1)S(1)} %get-tuple-element.39), channel_id=1, source_target_pairs={{0,3},{1,2},{2,1},{3,0},{4,7},{5,6},{6,5},{7,4},{8,11},{9,10},{10,... | collective-permute-start | bytes 540680 | tf_op jit(solution)/shard_map/ppermute | solution.py:328
  13.8 1.2 copy-start
  24.8 65.1 %all-to-all-start = ((bf16[64,64,256]{2,1,0:T(8,128)(2,1)}), bf16[64,64,256]{2,1,0:T(8,128)(2,1)S(1)}, u32[]{:S(2)}, u32[]{:S(2)}) async-start(bf16[64,64,256]{2,1,0:T(8,128)(2,1)} %shard_map.56), calls=%async_computation | async-start | bytes 4194304 | tf_op jit(solution)/shard_map/all_to_all | solution.py:372
  39.7 7.7 %collective-permute-start.5 = (bf16[256,384]{1,0:T(8,128)(2,1)}, bf16[256,384]{1,0:T(8,128)(2,1)S(1)}, u32[]{:S(2)}, u32[]{:S(2)}) collective-permute-start(bf16[256,384]{1,0:T(8,128)(2,1)} %get-tuple-element.43), channel_id=1, source_target_pairs={{0,8},{4,12},{8,0},{12,4},{1,9},{5,13},{9,1},{13,5},{2,10},{6,14},... | collective-permute-start | bytes 589832 | tf_op jit(solution)/shard_map/ppermute | solution.py:333
  42.5 9.3 %collective-permute-start.4 = (bf16[256,384]{1,0:T(8,128)(2,1)}, bf16[256,384]{1,0:T(8,128)(2,1)S(1)}, u32[]{:S(2)}, u32[]{:S(2)}) collective-permute-start(bf16[256,384]{1,0:T(8,128)(2,1)} %get-tuple-element.43), channel_id=1, source_target_pairs={{0,12},{4,0},{8,4},{12,8},{1,13},{5,1},{9,5},{13,9},{2,14},{6,2},{... | collective-permute-start | bytes 589832 | tf_op jit(solution)/shard_map/ppermute | solution.py:333
  43.3 8.5 %collective-permute-start.3 = (bf16[256,384]{1,0:T(8,128)(2,1)}, bf16[256,384]{1,0:T(8,128)(2,1)S(1)}, u32[]{:S(2)}, u32[]{:S(2)}) collective-permute-start(bf16[256,384]{1,0:T(8,128)(2,1)} %get-tuple-element.43), channel_id=1, source_target_pairs={{0,4},{4,8},{8,12},{12,0},{1,5},{5,9},{9,13},{13,1},{2,6},{6,10},{... | collective-permute-start | bytes 589832 | tf_op jit(solution)/shard_map/ppermute | solution.py:333
  54.5 1.3 copy-start.3
  55.9 1.0 copy-start.5
  56.9 0.8 copy-start.7
  90.0 5.3 %copy-start.4 = (f32[2048,256]{1,0:T(8,128)S(1)}, f32[2048,256]{1,0:T(8,128)}, u32[]{:S(2)}) copy-start(f32[2048,256]{1,0:T(8,128)} %copy-done.3) | copy-start | bytes 6291460
  91.0 15.2 %collective-permute-start.6 = (bf16[1024,256]{1,0:T(8,128)(2,1)S(1)}, bf16[1024,256]{1,0:T(8,128)(2,1)S(1)}, u32[]{:S(2)}, u32[]{:S(2)}) collective-permute-start(bf16[1024,256]{1,0:T(8,128)(2,1)S(1)} %get-tuple-element.49.refs_0_), channel_id=1, source_target_pairs={{0,4},{4,8},{8,12},{12,0},{1,5},{5,9},{9,13},{13,1},{2,6},{6,10},{... | collective-permute-start | bytes 1572872 | tf_op jit(solution)/shard_map/ppermute | solution.py:333
  92.3 13.9 %collective-permute-start.7 = (bf16[1024,256]{1,0:T(8,128)(2,1)S(1)}, bf16[1024,256]{1,0:T(8,128)(2,1)S(1)}, u32[]{:S(2)}, u32[]{:S(2)}) collective-permute-start(bf16[1024,256]{1,0:T(8,128)(2,1)S(1)} %get-tuple-element.50.refs_1_), channel_id=1, source_target_pairs={{0,12},{4,0},{8,4},{12,8},{1,13},{5,1},{9,5},{13,9},{2,14},{6,2},{... | collective-permute-start | bytes 1572872 | tf_op jit(solution)/shard_map/ppermute | solution.py:333
  93.7 23.7 %collective-permute-start.9 = (bf16[1024,256]{1,0:T(8,128)(2,1)S(1)}, bf16[1024,256]{1,0:T(8,128)(2,1)S(1)}, u32[]{:S(2)}, u32[]{:S(2)}) collective-permute-start(bf16[1024,256]{1,0:T(8,128)(2,1)S(1)} %get-tuple-element.49.refs_0_), channel_id=1, source_target_pairs={{0,12},{4,0},{8,4},{12,8},{1,13},{5,1},{9,5},{13,9},{2,14},{6,2},{... | collective-permute-start | bytes 1572872 | tf_op jit(solution)/shard_map/ppermute | solution.py:333
  95.0 22.4 %collective-permute-start.8 = (bf16[1024,256]{1,0:T(8,128)(2,1)S(1)}, bf16[1024,256]{1,0:T(8,128)(2,1)S(1)}, u32[]{:S(2)}, u32[]{:S(2)}) collective-permute-start(bf16[1024,256]{1,0:T(8,128)(2,1)S(1)} %get-tuple-element.50.refs_1_), channel_id=1, source_target_pairs={{0,4},{4,8},{8,12},{12,0},{1,5},{5,9},{9,13},{13,1},{2,6},{6,10},{... | collective-permute-start | bytes 1572872 | tf_op jit(solution)/shard_map/ppermute | solution.py:333
  95.2 1.2 copy-start.6
  96.4 1.0 copy-start.8
  106.2 21.9 %collective-permute-start.10 = (bf16[1024,256]{1,0:T(8,128)(2,1)S(1)}, bf16[1024,256]{1,0:T(8,128)(2,1)S(1)}, u32[]{:S(2)}, u32[]{:S(2)}) collective-permute-start(bf16[1024,256]{1,0:T(8,128)(2,1)S(1)} %collective-permute-done.6.refs_0_), channel_id=1, source_target_pairs={{0,4},{4,8},{8,12},{12,0},{1,5},{5,9},{9,13},{13,1},{2,6},{6,10},{... | collective-permute-start | bytes 1572872 | tf_op jit(solution)/shard_map/ppermute | solution.py:333
  107.4 21.2 %collective-permute-start.11 = (bf16[1024,256]{1,0:T(8,128)(2,1)S(1)}, bf16[1024,256]{1,0:T(8,128)(2,1)S(1)}, u32[]{:S(2)}, u32[]{:S(2)}) collective-permute-start(bf16[1024,256]{1,0:T(8,128)(2,1)S(1)} %collective-permute-done.7.refs_1_), channel_id=1, source_target_pairs={{0,12},{4,0},{8,4},{12,8},{1,13},{5,1},{9,5},{13,9},{2,14},{6,2},{... | collective-permute-start | bytes 1572872 | tf_op jit(solution)/shard_map/ppermute | solution.py:333
  135.3 6.1 %collective-permute-start.12 = (bf16[64,1024]{1,0:T(8,128)(2,1)S(1)}, bf16[64,1024]{1,0:T(8,128)(2,1)S(1)}, u32[]{:S(2)}, u32[]{:S(2)}) collective-permute-start(bf16[64,1024]{1,0:T(8,128)(2,1)S(1)} %get-tuple-element.64), channel_id=1, source_target_pairs={{0,1},{1,0},{2,3},{3,2},{4,5},{5,4},{6,7},{7,6},{8,9},{9,8},{10,11... | collective-permute-start | bytes 393224 | tf_op jit(solution)/shard_map/ppermute | solution.py:328
  135.7 11.3 %collective-permute-start.13 = (bf16[64,1024]{1,0:T(8,128)(2,1)S(1)}, bf16[64,1024]{1,0:T(8,128)(2,1)S(1)}, u32[]{:S(2)}, u32[]{:S(2)}) collective-permute-start(bf16[64,1024]{1,0:T(8,128)(2,1)S(1)} %get-tuple-element.65), channel_id=1, source_target_pairs={{0,2},{1,3},{2,0},{3,1},{4,6},{5,7},{6,4},{7,5},{8,10},{9,11},{10,... | collective-permute-start | bytes 393224 | tf_op jit(solution)/shard_map/ppermute | solution.py:328
  138.0 14.2 %collective-permute-start.14 = (bf16[64,1024]{1,0:T(8,128)(2,1)S(1)}, bf16[64,1024]{1,0:T(8,128)(2,1)S(1)}, u32[]{:S(2)}, u32[]{:S(2)}) collective-permute-start(bf16[64,1024]{1,0:T(8,128)(2,1)S(1)} %get-tuple-element.66), channel_id=1, source_target_pairs={{0,3},{1,2},{2,1},{3,0},{4,7},{5,6},{6,5},{7,4},{8,11},{9,10},{10,... | collective-permute-start | bytes 393224 | tf_op jit(solution)/shard_map/ppermute | solution.py:328
